TPU v7x, 32 devices: a whole 2x2x4 slice. The times are simulated.
32 devices in a mesh: dp: 8 (over y, x, core), tensor: 4 (over z).
Axes of the slice: x: 2, y: 2, z: 4, core: 2. Of those that a mesh axis runs over, the one named last changes fastest.
Arguments:
- tokens: bfloat16 [32, 320, 1024], P('dp'), may hold values from -6 to 6
- lengths: int32 [32], P('dp'), may hold values from 65 to 320, as said below
- adapter_ids: int32 [32, 4], P('dp'), may hold values from 0 to 7
- qkv_weight: bfloat16 [1024, 3, 1024], P(None, None, 'tensor'), may hold values from -0.1875 to 0.1875
- qkv_down: bfloat16 [8, 1024, 16], replicated, may hold values from -0.1875 to 0.1875
- qkv_up: bfloat16 [8, 16, 3, 1024], P(None, None, None, 'tensor'), may hold values from -0.75 to 0.75
- out_weight: bfloat16 [1024, 1024], P('tensor'), may hold values from -1 to 1
- out_down: bfloat16 [8, 1024, 16], P(None, 'tensor'), may hold values from -1 to 1
- out_up: bfloat16 [8, 16, 1024], replicated, may hold values from -0.75 to 0.75
- fc1_weight: bfloat16 [1024, 4096], P(None, 'tensor'), may hold values from -0.1875 to 0.1875
- fc1_down: bfloat16 [8, 1024, 16], replicated, may hold values from -0.1875 to 0.1875
- fc1_up: bfloat16 [8, 16, 4096], P(None, None, 'tensor'), may hold values from -0.75 to 0.75
- fc2_weight: bfloat16 [4096, 1024], P('tensor'), may hold values from -0.09375 to 0.09375
- fc2_down: bfloat16 [8, 4096, 16], P(None, 'tensor'), may hold values from -0.09375 to 0.09375
- fc2_up: bfloat16 [8, 16, 1024], replicated, may hold values from -0.75 to 0.75
- cotangent: bfloat16 [32, 320, 1024], P('dp', None, 'tensor'), may hold values from -6 to 6
Outputs:
- output: float32 [32, 320, 1024], P('dp', None, 'tensor')
- input_grad: float32 [32, 320, 1024], P('dp', None, 'tensor')
- grad_qkv_down: float32 [8, 1024, 16], replicated
- grad_qkv_up: float32 [8, 16, 3, 1024], P(None, None, None, 'tensor')
- grad_out_down: float32 [8, 1024, 16], P(None, 'tensor')
- grad_out_up: float32 [8, 16, 1024], replicated
- grad_fc1_down: float32 [8, 1024, 16], replicated
- grad_fc1_up: float32 [8, 16, 4096], P(None, None, 'tensor')
- grad_fc2_down: float32 [8, 4096, 16], P(None, 'tensor')
- grad_fc2_up: float32 [8, 16, 1024], replicated
Inputs may be any that keep to these rules, and one draw needn't show every extreme that they name: `lengths`: each image's valid slots are its 64 buffer tokens and a prefix of its other slots; some image fills all 320 slots and some image has only one slot beyond its buffer. `adapter_ids`: columns name the adapter for the qkv, output, fc1 and fc2 projections, in that order.
All inputs are finite; a program needn't handle non-finite values.
Results may differ from a plain program's by a relative error of at most 0.015.
Values may be sent and summed in bfloat16 or wider, within the bound.
A program may use at most 192 MiB of HBM per device.

v0:
```python
import jax
import jax.numpy as jnp
from jax import lax
from jax.sharding import PartitionSpec as P

HD = 64


EPSILON = 1e-06
NEG_FILL = -1e30


def norm_rows(values):
    centred = values - jnp.mean(values, axis=-1, keepdims=True)
    return centred * lax.rsqrt(jnp.mean(centred * centred, axis=-1, keepdims=True) + EPSILON)


def smooth_gate(values):
    return jax.nn.gelu(values, approximate=False)


def product(left, right):
    return jnp.dot(left, right, preferred_element_type=jnp.float32)


def product_left(left, right):
    return lax.dot_general(
        left, right, (((0,), (0,)), ((), ())), preferred_element_type=jnp.float32
    )


def product_right(left, right):
    return lax.dot_general(
        left, right, (((1,), (1,)), ((), ())), preferred_element_type=jnp.float32
    )


def flat_down(down):
    return jnp.transpose(down, (1, 0, 2)).reshape(down.shape[1], down.shape[0] * down.shape[2])


def split_down(gradient, adapter_count):
    return jnp.transpose(gradient.reshape(gradient.shape[0], adapter_count, -1), (1, 0, 2))


def adapter_masks(adapter_ids, adapter_count, rank_size, slot_count):
    owners = jnp.arange(adapter_count * rank_size, dtype=jnp.int32) // rank_size
    selectors = []
    for column in range(4):
        picked = (adapter_ids[:, column][:, None] == owners[None, :]).astype(jnp.float32)
        spread = jnp.broadcast_to(
            picked[:, None, :], (picked.shape[0], slot_count, picked.shape[1])
        )
        selectors.append(spread.reshape(picked.shape[0] * slot_count, picked.shape[1]))
    return selectors


def shards(
    tokens,
    lengths,
    adapter_ids,
    qkv_weight,
    qkv_down,
    qkv_up,
    out_weight,
    out_down,
    out_up,
    fc1_weight,
    fc1_down,
    fc1_up,
    fc2_weight,
    fc2_down,
    fc2_up,
    cotangent,
):
    seq_count, slot_count, model_width = tokens.shape
    adapter_count = qkv_down.shape[0]
    rank_size = qkv_down.shape[2]
    total_rank = adapter_count * rank_size
    local_width = out_weight.shape[0]
    heads_here = local_width // HD
    row_count = seq_count * slot_count
    column_count = cotangent.shape[2]
    column_start = lax.axis_index("tensor") * column_count
    scaling = HD ** (-0.5)
    inputs = tokens.reshape(row_count, model_width).astype(jnp.float32)
    positions = jnp.arange(slot_count, dtype=jnp.int32)
    valid = positions[None, :] < lengths[:, None]
    keep_rows = valid.reshape(row_count, 1).astype(jnp.float32)
    key_valid = valid[:, None, None, :]
    selectors = adapter_masks(adapter_ids, adapter_count, rank_size, slot_count)
    qkv_low = flat_down(qkv_down)
    out_low = flat_down(out_down)
    fc1_low = flat_down(fc1_down)
    fc2_low = flat_down(fc2_down)
    qkv_lift = qkv_up.reshape(total_rank, 3 * local_width)
    out_lift = out_up.reshape(total_rank, model_width)
    fc1_lift = fc1_up.reshape(total_rank, fc1_up.shape[2])
    fc2_lift = fc2_up.reshape(total_rank, model_width)
    qkv_cat = qkv_weight.reshape(model_width, 3 * local_width)
    first_vals, first_back = jax.vjp(norm_rows, inputs)
    first_in = first_vals.astype(jnp.bfloat16)
    lift_qkv = (selectors[0] * product(first_in, qkv_low)).astype(jnp.bfloat16)
    projected = (product(first_in, qkv_cat) + product(lift_qkv, qkv_lift)).astype(jnp.bfloat16)
    projected = projected.reshape(seq_count, slot_count, 3, heads_here, HD)
    queries = projected[:, :, 0]
    key_rows = projected[:, :, 1]
    value_rows = projected[:, :, 2]

    def masked_scores():
        scores = (
            jnp.einsum("slhd,smhd->shlm", queries, key_rows, preferred_element_type=jnp.float32)
            * scaling
        )
        return jnp.where(key_valid, scores, NEG_FILL)

    masked = masked_scores()
    peak = jnp.max(masked, axis=-1, keepdims=True)
    log_total = peak + jnp.log(jnp.sum(jnp.exp(masked - peak), axis=-1, keepdims=True))
    soft_weights = jnp.exp(masked - log_total)
    attended = jnp.einsum(
        "shlm,smhd->slhd",
        soft_weights.astype(jnp.bfloat16),
        value_rows,
        preferred_element_type=jnp.float32,
    )
    attended = attended.astype(jnp.bfloat16).reshape(row_count, local_width)
    part_out = product(attended, out_weight)
    part_lift = product(attended, out_low)
    out_total, lift_total = lax.psum((part_out, part_lift), "tensor")
    lift_out = (selectors[1] * lift_total).astype(jnp.bfloat16)
    mixed_rows = inputs + (out_total + product(lift_out, out_lift))
    second_vals, second_back = jax.vjp(norm_rows, mixed_rows)
    second_in = second_vals.astype(jnp.bfloat16)
    lift_fc1 = (selectors[2] * product(second_in, fc1_low)).astype(jnp.bfloat16)
    before = product(second_in, fc1_weight) + product(lift_fc1, fc1_lift)
    gate_vals, gate_back = jax.vjp(smooth_gate, before)
    hidden = gate_vals.astype(jnp.bfloat16)
    lift_partial = product(hidden, fc2_low)
    lift_fc2 = (selectors[3] * lax.psum(lift_partial, "tensor")).astype(jnp.bfloat16)
    block_cols = lax.psum_scatter(
        product(hidden, fc2_weight).astype(jnp.bfloat16), "tensor", scatter_dimension=1, tiled=True
    ).astype(jnp.float32)
    lift_cols = lax.dynamic_slice_in_dim(fc2_lift, column_start, column_count, 1)
    mixed_cols = lax.dynamic_slice_in_dim(mixed_rows, column_start, column_count, 1)
    output = keep_rows * (mixed_cols + block_cols + product(lift_fc2, lift_cols))
    cot_full = lax.all_gather(
        cotangent.reshape(row_count, column_count), "tensor", axis=1, tiled=True
    )
    grad_out_full = keep_rows * cot_full.astype(jnp.float32)
    grad_out_in = grad_out_full.astype(jnp.bfloat16)
    grad_lift_fc2 = (selectors[3] * product_right(grad_out_in, fc2_lift)).astype(jnp.bfloat16)
    grad_fc2_up = product_left(lift_fc2, grad_out_in).reshape(adapter_count, rank_size, model_width)
    grad_fc2_down = split_down(product_left(hidden, grad_lift_fc2), adapter_count)
    grad_hidden = product_right(grad_out_in, fc2_weight) + product_right(grad_lift_fc2, fc2_low)
    grad_before = gate_back(grad_hidden)[0].astype(jnp.bfloat16)
    grad_fc1_up = product_left(lift_fc1, grad_before).reshape(
        adapter_count, rank_size, fc1_up.shape[2]
    )
    part_second = product_right(grad_before, fc1_weight)
    part_lift_fc1 = product_right(grad_before, fc1_lift)
    sum_second, sum_lift_fc1 = lax.psum((part_second, part_lift_fc1), "tensor")
    grad_lift_fc1 = (selectors[2] * sum_lift_fc1).astype(jnp.bfloat16)
    grad_fc1_down = split_down(product_left(second_in, grad_lift_fc1), adapter_count)
    grad_second = sum_second + product_right(grad_lift_fc1, fc1_low)
    grad_mixed = grad_out_full + second_back(grad_second)[0]
    grad_branch = grad_mixed.astype(jnp.bfloat16)
    grad_out_up = product_left(lift_out, grad_branch).reshape(adapter_count, rank_size, model_width)
    grad_lift_out = (selectors[1] * product_right(grad_branch, out_lift)).astype(jnp.bfloat16)
    grad_out_down = split_down(product_left(attended, grad_lift_out), adapter_count)
    grad_attended = product_right(grad_branch, out_weight) + product_right(grad_lift_out, out_low)
    grad_attended = grad_attended.astype(jnp.bfloat16).reshape(
        seq_count, slot_count, heads_here, HD
    )
    soft_again = jnp.exp(masked_scores() - log_total)
    grad_values = jnp.einsum(
        "shlm,slhd->smhd",
        soft_again.astype(jnp.bfloat16),
        grad_attended,
        preferred_element_type=jnp.float32,
    )
    grad_soft = jnp.einsum(
        "slhd,smhd->shlm", grad_attended, value_rows, preferred_element_type=jnp.float32
    )
    weighted = jnp.sum(soft_again * grad_soft, axis=-1, keepdims=True)
    grad_scores = (soft_again * (grad_soft - weighted)).astype(jnp.bfloat16)
    grad_queries = (
        jnp.einsum("shlm,smhd->slhd", grad_scores, key_rows, preferred_element_type=jnp.float32)
        * scaling
    )
    grad_keys = (
        jnp.einsum("shlm,slhd->smhd", grad_scores, queries, preferred_element_type=jnp.float32)
        * scaling
    )
    grad_projected = jnp.stack([grad_queries, grad_keys, grad_values], axis=2).astype(jnp.bfloat16)
    grad_projected = grad_projected.reshape(row_count, 3 * local_width)
    grad_qkv_up = product_left(lift_qkv, grad_projected).reshape(
        adapter_count, rank_size, 3, local_width
    )
    part_lift_qkv = product_right(grad_projected, qkv_lift)
    sum_lift_qkv = lax.psum(part_lift_qkv, "tensor")
    grad_lift_qkv = (selectors[0] * sum_lift_qkv).astype(jnp.bfloat16)
    grad_qkv_down = split_down(product_left(first_in, grad_lift_qkv), adapter_count)
    own_part = first_back(product_right(grad_projected, qkv_cat))[0]
    shared_part = first_back(product_right(grad_lift_qkv, qkv_low))[0] + grad_mixed
    grad_cols = lax.psum_scatter(
        own_part.astype(jnp.bfloat16), "tensor", scatter_dimension=1, tiled=True
    ).astype(jnp.float32)
    input_grad = grad_cols + lax.dynamic_slice_in_dim(shared_part, column_start, column_count, 1)
    (
        grad_qkv_down,
        grad_qkv_up,
        grad_out_down,
        grad_out_up,
        grad_fc1_down,
        grad_fc1_up,
        grad_fc2_down,
        grad_fc2_up,
    ) = lax.psum(
        (
            grad_qkv_down,
            grad_qkv_up,
            grad_out_down,
            grad_out_up,
            grad_fc1_down,
            grad_fc1_up,
            grad_fc2_down,
            grad_fc2_up,
        ),
        "dp",
    )
    return (
        output.reshape(seq_count, slot_count, column_count),
        input_grad.reshape(seq_count, slot_count, column_count),
        grad_qkv_down,
        grad_qkv_up,
        grad_out_down,
        grad_out_up,
        grad_fc1_down,
        grad_fc1_up,
        grad_fc2_down,
        grad_fc2_up,
    )


def solution(mesh):
    in_specs = (
        P("dp", None, None),
        P("dp"),
        P("dp", None),
        P(None, None, "tensor"),
        P(),
        P(None, None, None, "tensor"),
        P("tensor", None),
        P(None, "tensor", None),
        P(),
        P(None, "tensor"),
        P(),
        P(None, None, "tensor"),
        P("tensor", None),
        P(None, "tensor", None),
        P(),
        P("dp", None, "tensor"),
    )
    out_specs = (
        P("dp", None, "tensor"),
        P("dp", None, "tensor"),
        P(),
        P(None, None, None, "tensor"),
        P(None, "tensor", None),
        P(),
        P(),
        P(None, None, "tensor"),
        P(None, "tensor", None),
        P(),
    )
    return jax.shard_map(shards, mesh=mesh, in_specs=in_specs, out_specs=out_specs, check_vma=False)
```

profile of v0, /device:TPU:0, one launch (start us, length us, event | category | flops | bytes accessed | tf_op | source)
XLA Modules:
  0.0 835.3 jit_solution(370719123321173907)
XLA Ops:
  19.3 6.5 fusion.67
  33.6 6.7 reshape.413
  40.3 4.0 fusion.65
  46.7 3.5 copy.102
  50.3 3.2 copy.100
  54.1 3.2 fusion
  64.9 4.2 fusion.68
  72.8 7.7 fusion.59
  80.5 202.0 %all-reduce.15.cloned.1.call-done = (f32[1280,1024]{1,0:T(8,128)}, f32[1280,128]{1,0:T(8,128)}) async-done(((f32[1280,1024]{1,0:T(8,128)}, f32[1280,128]{1,0:T(8,128)}), (f32[1280,1024]{1,0:T(8,128)}, f32[1280,128]{1,0:T(8,128)})) %all-reduce.15.cloned.1.call-update) | async-done | bytes 5898256 | tf_op jit(solution)/shard_map/psum | solution.py:130
  283.6 4.4 fusion.66
  294.4 13.6 %multiply_convert_fusion.1 = (bf16[1280,1024]{1,0:T(8,128)(2,1)}, f32[1280,1024]{1,0:T(8,128)S(1)}, f32[1280,1024]{1,0:T(8,128)S(1)}) fusion(f32[1280,1024]{1,0:T(8,128)S(1)} %fusion.70, bf16[1280,128]{1,0:T(8,128)(2,1)S(1)} %fusion.23, bf16[128,1024]{1,0:T(8,128)(2,1)S(1)} %bitcast.234), kind=kOutput, calls=%fused_computation.31 | convolution fusion | flops 422051840 | bytes 18939904 | tf_op jit(solution)/shard_map/dot_general | solution.py:23
  310.7 4.7 fusion.72
  317.3 3.5 fusion.71
  320.8 206.0 %all-reduce.13.cloned.1.call-done = (f32[1280,1024]{1,0:T(8,128)}, f32[1280,128]{1,0:T(8,128)}) async-done(((f32[1280,1024]{1,0:T(8,128)}, f32[1280,128]{1,0:T(8,128)}), (f32[1280,1024]{1,0:T(8,128)}, f32[1280,128]{1,0:T(8,128)})) %all-reduce.13.cloned.1.call-update) | async-done | bytes 5898256 | tf_op jit(solution)/shard_map/psum | solution.py:162
  527.9 5.4 multiply_reduce_fusion.1
  541.7 6.1 multiply_reduce_fusion
  547.8 4.8 multiply_convert_fusion
  558.0 3.2 copy.81
  561.2 3.7 convert_element_type.184
  566.6 6.8 convolution_convert_fusion
  573.6 52.3 %all-reduce.11.cloned.1.call-done = (f32[1280,128]{1,0:T(8,128)}, f32[1280,128]{1,0:T(8,128)}) async-done(((f32[1280,128]{1,0:T(8,128)}, f32[1280,128]{1,0:T(8,128)}), (f32[1280,128]{1,0:T(8,128)}, f32[1280,128]{1,0:T(8,128)})) %all-reduce.11.cloned.1.call-update) | async-done | bytes 1310736 | tf_op jit(solution)/shard_map/psum | solution.py:140
  630.0 3.3 fusion.10
  633.3 4.7 fusion.62
  640.2 3.1 fusion.78
  643.4 3.3 fusion.79
  652.3 3.2 fusion.77
  657.1 3.3 fusion.56
  660.3 3.0 convolution_bitcast_fusion.1
  663.4 16.5 %reduce-scatter.3.cloned.1.call-done = bf16[1280,256]{1,0:T(8,128)(2,1)} async-done(((bf16[1280,1024]{1,0:T(8,128)(2,1)}), bf16[1280,256]{1,0:T(8,128)(2,1)}) %reduce-scatter.3.cloned.1.call-update) | async-done | bytes 655376 | tf_op jit(solution)/shard_map/reduce_scatter | solution.py:141
  682.8 51.0 %reduce-scatter.5.cloned.1.call-done = bf16[1280,256]{1,0:T(8,128)(2,1)} async-done(((bf16[1280,1024]{1,0:T(8,128)(2,1)}), bf16[1280,256]{1,0:T(8,128)(2,1)}) %reduce-scatter.5.cloned.1.call-update) | async-done | bytes 655376 | tf_op jit(solution)/shard_map/reduce_scatter | solution.py:206
  733.9 3.3 fusion.26
  737.2 78.4 %all-reduce.9.cloned.1.call-done = (f32[8,1024,16]{1,2,0:T(8,128)}, f32[8,16,3,256]{3,1,2,0:T(8,128)}, f32[8,256,16]{1,2,0:T(8,128)}, f32[8,16,1024]{2,1,0:T(8,1...) async-done(((f32[8,1024,16]{1,2,0:T(8,128)}, f32[8,16,3,256]{3,1,2,0:T(8,128)}, ...) | async-done | bytes 3670032 | tf_op jit(solution)/shard_map/psum | solution.py:219
  (216 shorter events, 91.3 us)
Async XLA Ops:
  7.2 283.3 %copy-start = (bf16[1024,1024]{1,0:T(8,128)(2,1)S(1)}, bf16[1024,1024]{1,0:T(8,128)(2,1)}, u32[]{:S(2)}) copy-start(bf16[1024,1024]{1,0:T(8,128)(2,1)} %param.25) | copy-start | bytes 6291460
  7.2 62.7 %all-gather.2.cloned.1.call-start = ((), (), s32[]{:S(2)}) async-start(), calls=%async_computation.3 | async-start | bytes 3276800 | tf_op jit(solution)/shard_map/all_gather | solution.py:147
  7.9 274.5 %all-reduce.15.cloned.1.call-start = ((), (), s32[]{:S(2)}) async-start(), calls=%async_computation.8 | async-start | bytes 11796480 | tf_op jit(solution)/shard_map/psum | solution.py:130
  8.0 6.5 copy-start.5
  26.5 7.1 copy-start.47
  40.3 13.2 %copy-start.52 = (s32[4]{0:T(128)S(1)}, s32[4]{0:T(128)}, u32[]{:S(2)}) copy-start(s32[4]{0:T(128)} %param.17) | copy-start | bytes 52
  46.7 10.6 %copy-start.11 = (bf16[4,320,1,4,64]{1,4,3,0,2:T(8,128)(2,1)}, bf16[4,320,1,4,64]{1,4,3,0,2:T(8,128)(2,1)S(1)}, u32[]{:S(2)}) copy-start(bf16[4,320,1,4,64]{1,4,3,0,2:T(8,128)(2,1)S(1)} %copy.101) | copy-start | bytes 1966084
  69.2 457.6 %all-reduce.13.cloned.1.call-start = ((), (), s32[]{:S(2)}) async-start(), calls=%async_computation.7 | async-start | bytes 11796480 | tf_op jit(solution)/shard_map/psum | solution.py:162
  72.7 235.3 %copy-start.38 = (bf16[1280,128]{1,0:T(8,128)(2,1)}, bf16[1280,128]{1,0:T(8,128)(2,1)S(1)}, u32[]{:S(2)}) copy-start(bf16[1280,128]{1,0:T(8,128)(2,1)S(1)} %fusion.24) | copy-start | bytes 983044
  72.8 209.7 %copy-start.49 = (f32[4,128]{1,0:T(4,128)S(1)}, f32[4,128]{1,0:T(4,128)}, u32[]{:S(2)}) copy-start(f32[4,128]{1,0:T(4,128)} %get-tuple-element.49) | copy-start | bytes 6148
  72.8 210.9 %copy-start.32 = (bf16[8,16,1024]{2,1,0:T(8,128)(2,1)S(1)}, bf16[8,16,1024]{2,1,0:T(8,128)(2,1)}, u32[]{:S(2)}) copy-start(bf16[8,16,1024]{2,1,0:T(8,128)(2,1)} %param.24) | copy-start | bytes 786436
  293.5 14.6 %slice-start.6 = ((s8[5242880]{0:T(1024)(128)(4,1)}), s8[1048576]{0:T(1024)(128)(4,1)S(1)}, s32[]{:S(2)}) async-start(s8[5242880]{0:T(1024)(128)(4,1)} %bitcast.246), calls=%async_computation.15 | async-start | bytes 2097152
  294.3 13.7 %copy-start.25 = (bf16[1280,128]{1,0:T(8,128)(2,1)}, bf16[1280,128]{1,0:T(8,128)(2,1)S(1)}, u32[]{:S(2)}) copy-start(bf16[1280,128]{1,0:T(8,128)(2,1)S(1)} %fusion.23) | copy-start | bytes 983044
  294.4 13.7 %copy-start.41 = (bf16[8,1024,16]{1,2,0:T(8,128)(2,1)S(1)}, bf16[8,1024,16]{1,2,0:T(8,128)(2,1)}, u32[]{:S(2)}) copy-start(bf16[8,1024,16]{1,2,0:T(8,128)(2,1)} %param.29) | copy-start | bytes 786436
  294.4 13.7 %slice-start.7 = ((s8[5242880]{0:T(1024)(128)(4,1)}), s8[4194304]{0:T(1024)(128)(4,1)S(1)}, s32[]{:S(2)}) async-start(s8[5242880]{0:T(1024)(128)(4,1)} %bitcast.246), calls=%async_computation.16 | async-start | bytes 8388608
  317.2 308.7 %all-reduce.11.cloned.1.call-start = ((), (), s32[]{:S(2)}) async-start(), calls=%async_computation.6 | async-start | bytes 2621440 | tf_op jit(solution)/shard_map/psum | solution.py:140
  317.2 216.1 %slice-start = ((s8[5242880]{0:T(1024)(128)(4,1)}), s8[1048576]{0:T(1024)(128)(4,1)S(1)}, s32[]{:S(2)}) async-start(s8[5242880]{0:T(1024)(128)(4,1)} %bitcast.194), calls=%async_computation.9 | async-start | bytes 2097152
  541.7 13.3 %slice-start.2 = ((s8[7864320]{0:T(1024)(128)(4,1)}), s8[4194304]{0:T(1024)(128)(4,1)S(1)}, s32[]{:S(2)}) async-start(s8[7864320]{0:T(1024)(128)(4,1)} %bitcast.196), calls=%async_computation.11 | async-start | bytes 8388608
  547.8 7.3 slice-start.3
  558.0 6.9 copy-start.29
  566.5 7.0 copy-start.45
  566.5 59.4 %copy-start.48 = (f32[4,128]{1,0:T(4,128)S(1)}, f32[4,128]{1,0:T(4,128)}, u32[]{:S(2)}) copy-start(f32[4,128]{1,0:T(4,128)} %copy-done.47) | copy-start | bytes 6148
  566.5 61.3 %copy-start.34 = (bf16[8,1024,16]{1,2,0:T(8,128)(2,1)S(1)}, bf16[8,1024,16]{1,2,0:T(8,128)(2,1)}, u32[]{:S(2)}) copy-start(bf16[8,1024,16]{1,2,0:T(8,128)(2,1)} %param.20) | copy-start | bytes 786436
  566.5 113.4 %reduce-scatter.3.cloned.1.call-start = ((), (), s32[]{:S(2)}) async-start(), calls=%async_computation.2 | async-start | bytes 3276800 | tf_op jit(solution)/shard_map/reduce_scatter | solution.py:141
  573.4 160.5 %reduce-scatter.5.cloned.1.call-start = ((), (), s32[]{:S(2)}) async-start(), calls=%async_computation.4 | async-start | bytes 3276800 | tf_op jit(solution)/shard_map/reduce_scatter | solution.py:206
  639.9 10.8 %copy-start.15 = (bf16[1280,128]{0,1:T(8,128)(2,1)S(1)}, bf16[1280,128]{0,1:T(8,128)(2,1)}, u32[]{:S(2)}) copy-start(bf16[1280,128]{0,1:T(8,128)(2,1)} %copy-done.14) | copy-start | bytes 983044
  639.9 175.7 %all-reduce.9.cloned.1.call-start = ((), (), s32[]{:S(2)}) async-start(), calls=%async_computation.5 | async-start | bytes 7340032 | tf_op jit(solution)/shard_map/psum | solution.py:219
  643.4 12.1 %slice-start.4 = ((s8[5242880]{0:T(1024)(128)(4,1)}), s8[1048576]{0:T(1024)(128)(4,1)S(1)}, s32[]{:S(2)}) async-start(s8[5242880]{0:T(1024)(128)(4,1)} %bitcast.198), calls=%async_computation.13 | async-start | bytes 2097152
  648.5 7.0 copy-start.22
  733.9 94.3 %copy-start.1 = (bf16[1024,1024]{1,0:T(8,128)(2,1)S(1)}, bf16[1024,1024]{1,0:T(8,128)(2,1)}, u32[]{:S(2)}) copy-start(bf16[1024,1024]{1,0:T(8,128)(2,1)} %param.25) | copy-start | bytes 6291460
  815.6 11.0 %copy-start.37 = (f32[8,1024,16]{1,2,0:T(8,128)S(1)}, f32[8,1024,16]{1,2,0:T(8,128)}, u32[]{:S(2)}) copy-start(f32[8,1024,16]{1,2,0:T(8,128)} %get-tuple-element.72) | copy-start | bytes 1572868
  815.6 11.8 %copy-start.36 = (f32[8,16,1024]{2,1,0:T(8,128)S(1)}, f32[8,16,1024]{2,1,0:T(8,128)}, u32[]{:S(2)}) copy-start(f32[8,16,1024]{2,1,0:T(8,128)} %get-tuple-element.73) | copy-start | bytes 1572868
  (36 other events, 103.3 us)
Sparse Core Ops, SparseCore 0:
  9.6 57.5 all-gather.1
  70.2 212.2 all-reduce.14
  317.3 209.4 all-reduce.12
  566.6 59.2 all-reduce.10
  628.1 51.7 reduce-scatter.2
  682.1 51.7 reduce-scatter.4
  739.2 76.4 all-reduce.8
where the time goes:
time: 839 us; the launch traced here: 835 us
  waiting for transfers between devices  607 us (72%)
  matrix products  122 us (15%)
  local copies, waits for them, and re-layouts  56.4 us (7%)
  other arithmetic  33.4 us (4%)
  between operations  15.3 us (2%)
    psum x1, waiting for transfers between devices, shards(): sum_second, sum_lift_fc1 = lax.psum((part_second, part_lift_fc1), 'tensor')  206 us
    psum x1, waiting for transfers between devices, shards(): out_total, lift_total = lax.psum((part_out, part_lift), 'tensor')  202 us
    psum x1, waiting for transfers between devices, shards(): lax.psum((grad_qkv_down, grad_qkv_up, grad_out_down, grad_out_up, grad_fc...  78.4 us
    dot_general x12, matrix products, product(): return jnp.dot(left, right, preferred_element_type=jnp.float32)  52.7 us
    psum x1, waiting for transfers between devices, shards(): lax.psum(lift_partial, 'tensor')  52.3 us
    reduce_scatter x1, waiting for transfers between devices, shards(): lax.psum_scatter(own_part.astype(jnp.bfloat16), 'tensor', scatter_dimensi...  51 us
    dot_general x12, matrix products, product_right(): lax.dot_general(left, right, (((1,), (1,)), ((), ())), preferred_element_...  32.7 us
    unnamed x136, local copies, waits for them, and re-layouts  32.1 us
  transfers between devices with their start and end apart: 7, of which 6 were waited for; matrix products, arithmetic and copies ran while one was open for 15% of the time, Pallas kernels for 0%

commit v1 on v0

v1 whole, which is shorter than its diff:
```python
import jax
import jax.numpy as jnp
from jax import lax
from jax.experimental import pallas as pl
from jax.experimental.pallas import tpu as pltpu
from jax.sharding import PartitionSpec as P


BF = jnp.bfloat16
F32 = jnp.float32
MESH = pl.DeviceIdType.MESH
EPSILON = 1e-6
NEG_FILL = -1e30
HD = 64
GROUP = 8
BLOCK = 32
STEP = 512
ORDER = ((0, 1, 2, 3), (1, 2, 0, 3), (2, 1, 3, 0), (3, 2, 1, 0))


def dot(a, b):
    return lax.dot_general(a, b, (((1,), (0,)), ((), ())), preferred_element_type=F32)


def dot_nt(a, b):
    return lax.dot_general(a, b, (((1,), (1,)), ((), ())), preferred_element_type=F32)


def dot_tn(a, b):
    return lax.dot_general(a, b, (((0,), (0,)), ((), ())), preferred_element_type=F32)


def rows_loop(count, body, block=BLOCK):
    @pl.loop(0, count // block)
    def _(i):
        body(pl.ds(pl.multiple_of(i * block, block), block))


def moments(values):
    centred = values - jnp.mean(values, axis=-1, keepdims=True)
    inverse = lax.rsqrt(jnp.mean(centred * centred, axis=-1, keepdims=True) + EPSILON)
    return centred, inverse


def norm_back(values, grad):
    centred, inverse = moments(values)
    hat = centred * inverse
    return inverse * (
        grad - jnp.mean(grad, axis=-1, keepdims=True) - hat * jnp.mean(grad * hat, axis=-1, keepdims=True)
    )


def pick(position, table):
    out = 0
    for k, v in enumerate(table):
        if v:
            out = out + jnp.where(position == k, v, 0)
    return out


class Bag:
    pass


def prep(r):
    def body(rows):
        centred, inverse = moments(r.x[rows, :].astype(F32))
        r.first[rows, :] = (centred * inverse).astype(BF)

    rows_loop(r.S, body)


def prep_dz(r):
    def body(rows):
        keep = (lax.broadcasted_iota(jnp.int32, (BLOCK, 1), 0) + rows.start) < r.length
        for j in range(4):
            v = r.dzq[j, rows, :]
            r.dz[rows, r.W * j : r.W * (j + 1)] = jnp.where(keep, v, jnp.zeros_like(v))

    rows_loop(r.S, body)
    r.g_fc2[...] = dot_nt(r.dz[...], r.up_fc2[...]).astype(BF)


def attn_fwd(r, q, init):
    S, W = r.S, r.W
    for i in range(3):
        p = dot(r.first[...], r.wq[q, i]) + dot(r.lift_qkv[...], r.sel[q, :, i * W : (i + 1) * W])
        r.proj[q, i] = p.astype(BF)
    valid = lax.broadcasted_iota(jnp.int32, (S, S), 0) < r.length
    lane = lax.broadcasted_iota(jnp.int32, (S, 128), 1)

    @pl.loop(0, W // 128)
    def _(pair):
        cols = pl.ds(pl.multiple_of(pair * 128, 128), 128)
        qp = r.proj[q, 0, :, cols]
        kp = r.proj[q, 1, :, cols]
        vp = r.proj[q, 2, :, cols]
        res = []
        for h in range(2):
            qm = jnp.where((lane // HD) == h, qp, jnp.zeros_like(qp))
            st = jnp.where(valid, dot_nt(kp, qm) * (HD**-0.5), NEG_FILL)
            e = jnp.exp(st - jnp.max(st, axis=0, keepdims=True))
            soft = e * (1.0 / jnp.sum(e, axis=0, keepdims=True))
            r.soft[q * (W // HD) + pair * 2 + h] = soft
            res.append(dot_tn(soft.astype(BF), vp))
        r.att[q, :, cols] = jnp.where((lane // HD) == 0, res[0], res[1]).astype(BF)

    a = r.att[q]
    t = dot(a, r.wo[q])
    l = dot_nt(a, r.sel[q, :, 3 * W : 4 * W])
    if init:
        r.branch[...] = t
        r.lift_out_acc[...] = l
    else:
        r.branch[...] += t
        r.lift_out_acc[...] += l


def after_attn(r):
    r.lift_out[...] = r.lift_out_acc[...].astype(BF)
    r.branch[...] += dot(r.lift_out[...], r.up_out[...])

    def body(rows):
        mixed = r.x[rows, :].astype(F32) + r.branch[rows, :]
        r.mixed[rows, :] = mixed
        centred, inverse = moments(mixed)
        r.second[rows, :] = (centred * inverse).astype(BF)

    rows_loop(r.S, body)
    r.lift_fc1[...] = dot_nt(r.second[...], r.dn_fc1[...]).astype(BF)
    r.outacc[...] = jnp.zeros_like(r.outacc)
    r.gsec[...] = jnp.zeros_like(r.gsec)
    r.lift_fc2_acc[...] = jnp.zeros_like(r.lift_fc2_acc)
    r.glf1_acc[...] = jnp.zeros_like(r.glf1_acc)


def ffn_unit(r, q, u):
    W, FQ = r.W, r.FQ
    cols = pl.ds(u * STEP, STEP)
    up1 = r.sel[q, :, 4 * W + u * STEP : 4 * W + (u + 1) * STEP]
    dn2 = r.sel[q, :, 4 * W + FQ + u * STEP : 4 * W + FQ + (u + 1) * STEP]
    r.before[...] = dot(r.second[...], r.w1[q, :, cols]) + dot(r.lift_fc1[...], up1)
    r.gh[...] = dot_nt(r.dz[...], r.w2[q, cols, :]) + dot(r.g_fc2[...], dn2)

    def body(rows):
        b = r.before[rows, :]
        cdf = 0.5 * (1.0 + lax.erf(b * (0.5**0.5)))
        r.hidden[rows, :] = (b * cdf).astype(BF)
        slope = cdf + b * jnp.exp(-0.5 * b * b) * 0.3989422804014327
        r.gb[rows, :] = (slope * r.gh[rows, :]).astype(BF)

    rows_loop(r.S, body)
    h = r.hidden[...]
    g = r.gb[...]
    r.outacc[...] += dot(h, r.w2[q, cols, :])
    r.gsec[...] += dot_nt(g, r.w1[q, :, cols])
    r.lift_fc2_acc[...] += dot_nt(h, dn2)
    r.glf1_acc[...] += dot_nt(g, up1)
    r.gall[q, :, u * STEP : (u + 1) * STEP] = dot_tn(r.lift_fc1[...], g).astype(BF)
    r.gall[q, :, FQ + u * STEP : FQ + (u + 1) * STEP] = dot_tn(r.g_fc2[...], h).astype(BF)


def after_ffn_out(r):
    r.lift_fc2[...] = r.lift_fc2_acc[...].astype(BF)
    r.outacc[...] += dot(r.lift_fc2[...], r.up_fc2[...])

    def body(rows):
        keep = (lax.broadcasted_iota(jnp.int32, (BLOCK, 1), 0) + rows.start) < r.length
        r.out[rows, :] = jnp.where(keep, r.mixed[rows, :] + r.outacc[rows, :], 0.0).astype(BF)

    rows_loop(r.S, body)


def put_rep(r, value, base):
    v = value.astype(BF)
    for j in range(4):
        r.gall[j, :, base : base + r.W] = v[:, r.W * j : r.W * (j + 1)]


def after_ffn_back(r):
    g1 = r.glf1_acc[...].astype(BF)
    put_rep(r, dot_tn(r.lift_fc2[...], r.dz[...]), 2 * r.FQ + r.W)
    put_rep(r, dot_tn(g1, r.second[...]), 2 * r.FQ)
    r.gsec[...] += dot(g1, r.dn_fc1[...])

    def body(rows):
        g = r.dz[rows, :].astype(F32) + norm_back(r.mixed[rows, :], r.gsec[rows, :])
        r.mixed[rows, :] = g
        r.gbr[rows, :] = g.astype(BF)

    rows_loop(r.S, body)
    gbr = r.gbr[...]
    put_rep(r, dot_tn(r.lift_out[...], gbr), 2 * r.FQ + 2 * r.W)
    r.g_out[...] = dot_nt(gbr, r.up_out[...]).astype(BF)
    r.glq_acc[...] = jnp.zeros_like(r.glq_acc)
    r.gsec[...] = jnp.zeros_like(r.gsec)


def attn_back(r, q):
    S, W = r.S, r.W
    od = r.sel[q, :, 3 * W : 4 * W]
    late = r.early
    r.gall[q, :, late + 3 * W : late + 4 * W] = dot_tn(r.g_out[...], r.att[q]).astype(BF)
    r.ga[...] = (dot_nt(r.gbr[...], r.wo[q]) + dot(r.g_out[...], od)).astype(BF)
    lane = lax.broadcasted_iota(jnp.int32, (S, 128), 1)

    @pl.loop(0, W // 128)
    def _(pair):
        cols = pl.ds(pl.multiple_of(pair * 128, 128), 128)
        qp = r.proj[q, 0, :, cols]
        kp = r.proj[q, 1, :, cols]
        vp = r.proj[q, 2, :, cols]
        gp = r.ga[:, cols]
        gv, gq, gk = [], [], []
        for h in range(2):
            mine = (lane // HD) == h
            gm = jnp.where(mine, gp, jnp.zeros_like(gp))
            qm = jnp.where(mine, qp, jnp.zeros_like(qp))
            soft = r.soft[q * (W // HD) + pair * 2 + h]
            gv.append(dot(soft.astype(BF), gm))
            gs = dot_nt(vp, gm)
            ds = (soft * (gs - jnp.sum(soft * gs, axis=0, keepdims=True))).astype(BF)
            gk.append(dot(ds, qm))
            gq.append(dot_tn(ds, kp))
        sc = HD**-0.5
        r.gp[0, :, cols] = (jnp.where((lane // HD) == 0, gq[0], gq[1]) * sc).astype(BF)
        r.gp[1, :, cols] = ((gk[0] + gk[1]) * sc).astype(BF)
        r.gp[2, :, cols] = (gv[0] + gv[1]).astype(BF)

    for i in range(3):
        g = r.gp[i]
        r.gall[q, :, late + i * W : late + (i + 1) * W] = dot_tn(r.lift_qkv[...], g).astype(BF)
        r.glq_acc[...] += dot_nt(g, r.sel[q, :, i * W : (i + 1) * W])
        r.gsec[...] += dot_nt(g, r.wq[q, i])


def finish_grads(r):
    gq = r.glq_acc[...].astype(BF)
    put_rep(r, dot_tn(gq, r.first[...]), r.early + 4 * r.W)
    r.gsec[...] += dot(gq, r.dn_qkv[...])


def finish_rows(r):
    def body(rows):
        r.gin[rows, :] = (r.mixed[rows, :] + norm_back(r.x[rows, :].astype(F32), r.gsec[rows, :])).astype(BF)

    rows_loop(r.S, body)


class Stream:
    def __init__(self, r):
        self.r = r
        d = self.d = lax.axis_index("dp")
        self.z = lax.axis_index("tensor")
        m = self.m = d % GROUP
        self.base = d - m
        self.dx = d + 2 - 4 * ((m // 2) % 2)
        self.dy = d + 4 - 8 * (m // 4)
        self.ds = d + 1 - 2 * (m % 2)
        self.dd = self.dx + self.dy - d
        self.q = [pick(self.z, [ORDER[k][i] for k in range(4)]) for i in range(4)]
        self.units = [("A", p, i) for i in (1, 2, 3) for p in range(2)]
        self.units += [("B", p, i) for i in (1, 2, 3) for p in range(4)]

    def greet(self):
        bar = pltpu.get_barrier_semaphore()
        for k in range(1, GROUP):
            peer = self.base + (self.m + k) % GROUP
            pl.semaphore_signal(bar, inc=1, device_id=(peer, self.z), device_id_type=MESH)
        for k in range(1, 4):
            pl.semaphore_signal(bar, inc=1, device_id=(self.d, (self.z + k) % 4), device_id_type=MESH)

    def met(self):
        pl.semaphore_wait(pltpu.get_barrier_semaphore(), GROUP + 2)

    def parts(self, kind, p, q, d, half=None):
        r, m = self.r, d - self.base
        if half is None:
            a, c = pl.ds(pl.multiple_of(m * 128, 128), 128), pl.ds(0, r.D)
        else:
            a, c = pl.ds(pl.multiple_of(m * 128 + 64 * half, 64), 64), pl.ds(r.D // 2 * half, r.D // 2)
        if kind == "A":
            b = pl.ds(pl.multiple_of(p * 128 + m * 16, 16), 16)
            return (r.wq.at[q, :, a, pl.ds(128 * p, 128)], r.wo.at[q, b, c])
        b = pl.ds(pl.multiple_of(p * 256 + m * 32, 32), 32)
        return (r.w1.at[q, a, pl.ds(256 * p, 256)], r.w2.at[q, b, c])

    def own(self, kind, p):
        r, m = self.r, self.m
        a = pl.ds(pl.multiple_of(m * 128, 128), 128)
        if kind == "A":
            return (r.hq.at[:, a, pl.ds(128 * p, 128)], r.ho.at[pl.ds(pl.multiple_of(p * 128 + m * 16, 16), 16), :])
        return (r.h1.at[a, pl.ds(256 * p, 256)], r.h2.at[pl.ds(pl.multiple_of(p * 256 + m * 32, 32), 32), :])

    def send(self, srcs, dsts, sem, dev):
        for s, t in zip(srcs, dsts):
            pltpu.make_async_remote_copy(
                src_ref=s, dst_ref=t, send_sem=self.r.sends, recv_sem=sem, device_id=dev, device_id_type=MESH
            ).start()

    def wait(self, rows, sem):
        v = self.r.w2.at[0, pl.ds(0, rows), :]
        pltpu.make_async_copy(v, v, sem).wait()

    def index(self, kind, p, i):
        return (i - 1) * 2 + p if kind == "A" else 6 + (i - 1) * 4 + p

    def own_sends(self, kind, p):
        z, d = self.z, self.d
        src = self.own(kind, p)
        dst = self.parts(kind, p, z, d)
        for step, last in ((1, 3), (-1, 0)):
            i = pick(z, [ORDER[k + step].index(k) if 0 <= k + step <= 3 else 0 for k in range(4)])

            @pl.when(z != last)
            def _():
                self.send(src, dst, self.r.rz.at[self.index(kind, p, i)], (d, z + step))

    def z_stage(self, t):
        kind, p, i = self.units[t]
        z, d, r = self.z, self.d, self.r
        self.wait(64, r.rz.at[t])
        piece = self.parts(kind, p, self.q[i], d)
        for step in (1, -1):
            go, slot = [], []
            for k in range(4):
                quarter = ORDER[k][i]
                on = 0 <= k + step <= 3 and (quarter < k if step == 1 else quarter > k)
                go.append(int(on))
                slot.append(ORDER[k + step].index(quarter) if on else 0)
            if any(go):

                @pl.when(pick(z, go) == 1)
                def _():
                    self.send(piece, piece, r.rz.at[self.index(kind, p, pick(z, slot))], (d, z + step))

        self.send(piece, piece, r.rx.at[t], (self.dx, z))
        self.send(piece, piece, r.ry.at[t], (self.dy, z))
        self.send(piece, piece, r.rs.at[t], (self.ds, z))

    def xy_stage(self, t):
        kind, p, i = self.units[t]
        z, q, r = self.z, self.q[i], self.r
        for sem, frm, to, half in ((r.rx, self.dx, self.dy, 0), (r.ry, self.dy, self.dx, 1)):
            self.wait(64, sem.at[t])
            h = self.parts(kind, p, q, frm, half)
            self.send(h, h, r.rd.at[t], (to, z))
            w = self.parts(kind, p, q, frm)
            self.send(w, w, r.rs.at[t], (self.ds, z))

    def d_stage(self, t):
        kind, p, i = self.units[t]
        self.wait(64, self.r.rd.at[t])
        w = self.parts(kind, p, self.q[i], self.dd)
        self.send(w, w, self.r.rs.at[t], (self.ds, self.z))

    def s_stage(self, t):
        self.wait(256, self.r.rs.at[t])

    def finish_sends(self):
        counts = []
        for k in range(4):
            c = 6 * ((k < 3) + (k > 0))
            for kind, p, i in self.units:
                quarter = ORDER[k][i]
                c += int(quarter < k and k < 3) + int(quarter > k and k > 0)
            counts.append(c + 7 * len(self.units))

        @pl.loop(0, pick(self.z, counts))
        def _(i):
            self.wait(64, self.r.sends)


    def to_planes(self, view, target, send_sem, recv_sem):
        for k in range(1, 4):
            j = (self.z + k) % 4
            pltpu.make_async_remote_copy(
                src_ref=view(j), dst_ref=target, send_sem=send_sem, recv_sem=recv_sem, device_id=(self.d, j), device_id_type=MESH
            ).start()

    def to_group(self, view, target, send_sem, recv_sem):
        for k in range(1, GROUP):
            m = (self.m + k) % GROUP
            pltpu.make_async_remote_copy(
                src_ref=view(m), dst_ref=target, send_sem=send_sem, recv_sem=recv_sem, device_id=(self.base + m, self.z), device_id_type=MESH
            ).start()

    def done(self, ref, *sems):
        for s in sems:
            pltpu.make_async_copy(ref, ref, s).wait()


def one_hot(r, p, transposed):
    R, T, n = r.R, r.T, r.n_img
    shape = (T, n * R) if transposed else (n * R, T)
    a = lax.broadcasted_iota(jnp.int32, shape, 1 if transposed else 0)
    b = lax.broadcasted_iota(jnp.int32, shape, 0 if transposed else 1)
    owner = jnp.zeros(shape, jnp.int32)
    for i in range(n):
        owner = jnp.where(a // R == i, r.ids[i, p], owner)
    hit = (b // R == owner) & (a % R == b % R)
    return jnp.where(hit, 1.0, 0.0).astype(BF)


def choose(r, p, flat):
    shape = (r.R, r.T)
    a = lax.broadcasted_iota(jnp.int32, shape, 0)
    b = lax.broadcasted_iota(jnp.int32, shape, 1)
    hit = (b // r.R == r.my_ids[p]) & (a == b % r.R)
    return dot(jnp.where(hit, 1.0, 0.0).astype(BF), flat).astype(BF)


def kernel(names, sizes, *refs):
    r = Bag()
    for n, f in zip(names, refs):
        setattr(r, n, f)
    for n, v in sizes.items():
        setattr(r, n, v)
    c = Stream(r)
    z, d = c.z, c.d
    W, FQ, R, n = r.W, r.FQ, r.R, r.n_img
    E = r.early
    r.length = r.len[z]
    r.my_ids = [r.ids[z, p] for p in range(4)]
    c.greet()
    load = []

    def fetch(src, dst):
        cp = pltpu.make_async_copy(src, dst, r.loc.at[len(load)])
        cp.start()
        load.append(cp)
        return cp

    l_x = fetch(r.tokens.at[z], r.x)
    l_ad = [fetch(getattr(r, "h_" + k), getattr(r, k)) for k in ("aqd", "aqu", "aod", "a1u", "a2d", "aou", "a1d", "a2u")]
    l_q = fetch(r.hq, r.wq.at[z])
    l_o = fetch(r.ho, r.wo.at[z])
    l_1 = fetch(r.h1, r.w1.at[z])
    l_2 = fetch(r.h2, r.w2.at[z])
    l_c = fetch(r.cot.at[z], r.dzq.at[z])
    c.met()
    kinds = [("A", 0), ("A", 1)] + [("B", p) for p in range(4)]
    for k in kinds[:2]:
        c.own_sends(*k)
    for cp in l_ad:
        cp.wait()
    hot = one_hot(r, 0, False)
    for i in range(3):
        flat = r.aqu[:, i].reshape(r.T, W)
        r.selout[:, :, i * W : (i + 1) * W] = dot(hot, flat).astype(BF).reshape(n, R, W)
    r.selout[:, :, 3 * W : 4 * W] = dot(one_hot(r, 1, False), r.aod[...]).astype(BF).reshape(n, R, W)
    r.selout[:, :, 4 * W : 4 * W + FQ] = dot(one_hot(r, 2, False), r.a1u[...]).astype(BF).reshape(n, R, FQ)
    r.selout[:, :, 4 * W + FQ :] = dot(one_hot(r, 3, False), r.a2d[...]).astype(BF).reshape(n, R, FQ)
    c.to_planes(lambda j: r.selout.at[j], r.sel.at[z], r.misc.at[0], r.misc.at[1])
    r.sel[z] = r.selout[z]
    for k in kinds[2:4]:
        c.own_sends(*k)
    r.dn_qkv[...] = choose(r, 0, r.aqd[...])
    r.up_out[...] = choose(r, 1, r.aou[...])
    r.dn_fc1[...] = choose(r, 2, r.a1d[...])
    r.up_fc2[...] = choose(r, 3, r.a2u[...])
    l_x.wait()
    prep(r)
    r.lift_qkv[...] = dot_nt(r.first[...], r.dn_qkv[...]).astype(BF)
    l_q.wait()
    l_o.wait()

    N = len(c.units)
    LZ, LX, LD = 2, 1, 1
    lag = LZ + LX + LD
    work = {}

    def at(tick, f):
        work.setdefault(tick, []).append(f)

    at(0, lambda: attn_fwd(r, c.q[0], True))
    at(1 + lag, lambda: c.done(r.sel.at[pl.ds(0, 3)], r.misc.at[0], r.misc.at[1]))
    at(1 + lag, lambda: attn_fwd(r, c.q[1], False))
    at(3 + lag, lambda: attn_fwd(r, c.q[2], False))
    at(2 + lag, lambda: [c.done(r.dzq.at[pl.ds(0, 3)], r.misc.at[2], r.misc.at[3]), l_c.wait(), prep_dz(r)])
    at(5 + lag, lambda: attn_fwd(r, c.q[3], False))
    at(5 + lag, lambda: [after_attn(r), l_1.wait(), l_2.wait()])
    at(6 + lag, lambda: ffn_unit(r, c.q[0], 0))
    at(7 + lag, lambda: ffn_unit(r, c.q[0], 1))
    for i in (1, 2, 3):
        for u in range(2):
            last = 6 + (i - 1) * 4 + 2 * u + 1
            at(last + lag, lambda i=i, u=u: ffn_unit(r, c.q[i], u))
    at(0, lambda: [c.own_sends(*kinds[4]), c.own_sends(*kinds[5])])
    at(0, lambda: c.to_planes(lambda j: r.cot.at[j], r.dzq.at[z], r.misc.at[2], r.misc.at[3]))
    for t in range(N + lag):
        if t < N:
            c.z_stage(t)
        if 0 <= t - LZ < N:
            c.xy_stage(t - LZ)
        if 0 <= t - LZ - LX < N:
            c.d_stage(t - LZ - LX)
        if 0 <= t - lag < N:
            c.s_stage(t - lag)
        for f in work.get(t, ()):
            f()

    after_ffn_out(r)
    mine = pl.ds(pl.multiple_of(z * W, W), W)

    def cut(ref):
        return lambda j: ref.at[:, pl.ds(pl.multiple_of(j * W, W), W)]

    c.to_planes(cut(r.out), r.outr.at[z], r.misc.at[4], r.misc.at[5])
    k_out = fetch(r.out.at[:, mine], r.outr.at[z])
    after_ffn_back(r)

    stages = []

    def make_stages(lo, rep, hi, s, fs, fr):
        cols, reps, own = pl.ds(lo, hi - lo), pl.ds(rep, hi - rep), pl.ds(lo, rep - lo)
        sem = [r.misc.at[s + k] for k in range(10)]

        def one():
            c.to_planes(lambda j: r.gall.at[j, :, cols], r.sp.at[z, :, cols], sem[0], sem[1])
            r.sp[z, :, cols] = r.gall[z, :, cols]

        def two():
            c.done(r.sp.at[pl.ds(0, 3), :, cols], sem[0], sem[1])
            for a, b, p in r.blocks:
                if lo <= a < hi:
                    v = r.sp[:, :, a:b].reshape(n * R, b - a)
                    r.dense[:, a:b] = dot(one_hot(r, p, True), v).astype(BF)
            c.to_group(lambda m: r.dense.at[pl.ds(pl.multiple_of(m * R, R), R), cols], r.rsb.at[c.m, :, cols], sem[2], sem[3])
            r.rsb[c.m, :, cols] = r.dense[pl.ds(pl.multiple_of(c.m * R, R), R), cols]

        def three():
            c.done(r.rsb.at[pl.ds(0, GROUP - 1), :, cols], sem[2], sem[3])
            total = r.rsb[0, :, cols].astype(F32)
            for k in range(1, GROUP):
                total = total + r.rsb[k, :, cols].astype(F32)
            r.red[:, cols] = total.astype(BF)
            zc = pl.ds(fr, hi - rep)
            c.to_planes(lambda j: r.red.at[:, reps], r.zb.at[z, :, zc], sem[4], sem[5])
            r.zb[z, :, zc] = r.red[:, reps]
            c.to_group(lambda m: r.red.at[:, own], r.fin_s.at[c.m, :, pl.ds(fs, rep - lo)], sem[6], sem[7])
            fetch(r.red.at[:, own], r.fin_s.at[c.m, :, pl.ds(fs, rep - lo)])

        def four():
            zc = pl.ds(fr, hi - rep)
            c.done(r.zb.at[pl.ds(0, 3), :, zc], sem[4], sem[5])
            c.to_group(lambda m: r.zb.at[:, :, zc], r.fin_r.at[c.m, :, :, zc], sem[8], sem[9])
            fetch(r.zb.at[:, :, zc], r.fin_r.at[c.m, :, :, zc])

        def five():
            zc = pl.ds(fr, hi - rep)
            c.done(r.fin_s.at[pl.ds(0, GROUP - 1), :, pl.ds(fs, rep - lo)], sem[6], sem[7])
            c.done(r.fin_r.at[pl.ds(0, GROUP - 1), :, :, zc], sem[8], sem[9])

        return one, two, three, four, five

    early = make_stages(0, 2 * FQ, E, 8, 0, 0)
    late = make_stages(E, E + 4 * W, E + 5 * W, 18, 2 * FQ, 3 * W)
    early[0]()
    attn_back(r, 0)
    early[1]()
    attn_back(r, 1)
    early[2]()
    attn_back(r, 2)
    early[3]()
    attn_back(r, 3)
    finish_grads(r)
    late[0]()
    finish_rows(r)
    c.to_planes(cut(r.gin), r.ginr.at[z], r.misc.at[6], r.misc.at[7])
    k_in = fetch(r.gin.at[:, mine], r.ginr.at[z])
    late[1]()
    late[2]()
    late[3]()
    early[4]()
    c.done(r.outr.at[pl.ds(0, 3)], r.misc.at[4], r.misc.at[5])
    c.finish_sends()
    late[4]()
    c.done(r.ginr.at[pl.ds(0, 3)], r.misc.at[6], r.misc.at[7])
    for cp in load[len(l_ad) + 6 :]:
        cp.wait()


def spread(out_ref, gin_ref, fs_ref, fr_ref, output, input_grad, qd, qu, od, ou, f1d, f1u, f2d, f2u):
    W = out_ref.shape[2]
    FQ = f1u.shape[2]
    output[...] = out_ref[...].astype(F32)
    input_grad[...] = gin_ref[...].astype(F32)
    f1u[...] = fs_ref[:, :, :FQ].astype(F32)
    f2d[...] = fs_ref[:, :, FQ : 2 * FQ].astype(F32)
    for i in range(3):
        qu[:, i] = fs_ref[:, :, 2 * FQ + i * W : 2 * FQ + (i + 1) * W].astype(F32)
    od[...] = fs_ref[:, :, 2 * FQ + 3 * W :].astype(F32)
    for k, ref in enumerate((f1d, f2u, ou, qd)):
        for j in range(4):
            ref[:, :, W * j : W * (j + 1)] = fr_ref[:, j, :, W * k : W * (k + 1)].astype(F32)


def make_shards(groups):
    def shards(
        tokens, lengths, adapter_ids, qkv_weight, qkv_down, qkv_up, out_weight, out_down, out_up,
        fc1_weight, fc1_down, fc1_up, fc2_weight, fc2_down, fc2_up, cotangent,
    ):
        n, S, D = tokens.shape
        A, _, R = qkv_down.shape
        T = A * R
        W = out_weight.shape[0]
        FQ = fc1_weight.shape[1]
        early = 2 * FQ + 3 * W
        total = early + 5 * W
        blocks = (
            (0, FQ, 2), (FQ, 2 * FQ, 3), (2 * FQ, 2 * FQ + W, 2), (2 * FQ + W, 2 * FQ + 2 * W, 3), (2 * FQ + 2 * W, early, 1),
            (early, early + 3 * W, 0), (early + 3 * W, early + 4 * W, 1), (early + 4 * W, total, 0),
        )
        sizes = dict(n_img=n, S=S, D=D, R=R, T=T, W=W, FQ=FQ, early=early, blocks=blocks)

        def turned(a):
            return jnp.transpose(a, (0, 2, 1)).reshape(T, a.shape[1])

        args = dict(
            len=lengths, ids=adapter_ids, tokens=tokens, cot=cotangent,
            hq=jnp.transpose(qkv_weight, (1, 0, 2)), ho=out_weight, h1=fc1_weight, h2=fc2_weight,
            h_aqd=turned(qkv_down), h_aqu=jnp.transpose(qkv_up, (0, 2, 1, 3)), h_aod=turned(out_down),
            h_a1u=fc1_up.reshape(T, FQ), h_a2d=turned(fc2_down), h_aou=out_up.reshape(T, D),
            h_a1d=turned(fc1_down), h_a2u=fc2_up.reshape(T, D),
        )
        outs = dict(outr=(n, S, W), ginr=(n, S, W), fin_s=(GROUP, R, 2 * FQ + 4 * W), fin_r=(GROUP, 4, R, 4 * W))
        vm = dict(
            wq=((4, 3, D, W), BF), wo=((4, W, D), BF), w1=((4, D, FQ), BF), w2=((4, FQ, D), BF),
            aqd=((T, D), BF), aqu=((A, 3, R, W), BF), aod=((T, W), BF), a1u=((T, FQ), BF), a2d=((T, FQ), BF),
            aou=((T, D), BF), a1d=((T, D), BF), a2u=((T, D), BF),
            selout=((n, R, 4 * W + 2 * FQ), BF), sel=((4, R, 4 * W + 2 * FQ), BF),
            dn_qkv=((R, D), BF), up_out=((R, D), BF), dn_fc1=((R, D), BF), up_fc2=((R, D), BF),
            x=((S, D), BF), dzq=((4, S, W), BF), dz=((S, D), BF),
            first=((S, D), BF), lift_qkv=((S, R), BF), g_fc2=((S, R), BF), proj=((4, 3, S, W), BF),
            soft=((4 * W // HD, S, S), F32), att=((4, S, W), BF), branch=((S, D), F32), lift_out_acc=((S, R), F32),
            lift_out=((S, R), BF), mixed=((S, D), F32), second=((S, D), BF), lift_fc1=((S, R), BF), outacc=((S, D), F32),
            gsec=((S, D), F32), lift_fc2_acc=((S, R), F32), glf1_acc=((S, R), F32), before=((S, STEP), F32), gh=((S, STEP), F32),
            hidden=((S, STEP), BF), gb=((S, STEP), BF), lift_fc2=((S, R), BF), gbr=((S, D), BF), g_out=((S, R), BF),
            glq_acc=((S, R), F32), ga=((S, W), BF), gp=((3, S, W), BF), out=((S, D), BF), gin=((S, D), BF),
            gall=((4, R, total), BF), sp=((n, R, total), BF), dense=((T, total), BF), rsb=((GROUP, R, total), BF),
            red=((R, total), BF), zb=((4, R, 4 * W), BF),
        )
        units = 18
        sems = dict(rz=units, rx=units, ry=units, rd=units, rs=units, sends=None, loc=24, misc=28)
        names = list(args) + list(outs) + list(vm) + list(sems)
        anywhere = pl.BlockSpec(memory_space=pl.ANY)
        got = pl.pallas_call(
            lambda *refs: kernel(names, sizes, *refs),
            out_shape=tuple(jax.ShapeDtypeStruct(s, BF) for s in outs.values()),
            in_specs=[pl.BlockSpec(memory_space=pltpu.SMEM)] * 2 + [anywhere] * (len(args) - 2),
            out_specs=tuple([anywhere] * len(outs)),
            scratch_shapes=[pltpu.VMEM(s, t) for s, t in vm.values()]
            + [pltpu.SemaphoreType.DMA if k is None else pltpu.SemaphoreType.DMA((k,)) for k in sems.values()],
            compiler_params=pltpu.CompilerParams(collective_id=0, has_side_effects=True, vmem_limit_bytes=60 * 2**20),
        )(*args.values())
        outr, ginr, fin_s, fin_r = got
        if groups > 1:
            across = [[m + GROUP * g for g in range(groups)] for m in range(GROUP)]
            fin_s, fin_r = lax.psum((fin_s.astype(F32), fin_r.astype(F32)), "dp", axis_index_groups=across)
        full = (A, R, D)
        vmem = pl.BlockSpec(memory_space=pltpu.VMEM)
        shapes = ((n, S, W), (n, S, W), full, (A, 3, R, W), (A, R, W), full, full, (A, R, FQ), (A, R, FQ), full)
        output, input_grad, qd, qu, od, ou, f1d, f1u, f2d, f2u = pl.pallas_call(
            spread,
            out_shape=tuple(jax.ShapeDtypeStruct(s, F32) for s in shapes),
            in_specs=[vmem] * 4,
            out_specs=tuple([vmem] * len(shapes)),
            compiler_params=pltpu.CompilerParams(vmem_limit_bytes=40 * 2**20),
        )(outr, ginr, fin_s, fin_r)
        back = lambda a: jnp.transpose(a, (0, 2, 1))
        return (output, input_grad, back(qd), jnp.transpose(qu, (0, 2, 1, 3)), back(od), ou, back(f1d), f1u, back(f2d), f2u)

    return shards


def solution(mesh):
    in_specs = (
        P("dp", None, None), P("dp"), P("dp", None), P(None, None, "tensor"), P(), P(None, None, None, "tensor"),
        P("tensor", None), P(None, "tensor", None), P(), P(None, "tensor"), P(), P(None, None, "tensor"),
        P("tensor", None), P(None, "tensor", None), P(), P("dp", None, "tensor"),
    )
    out_specs = (
        P("dp", None, "tensor"), P("dp", None, "tensor"), P(), P(None, None, None, "tensor"), P(None, "tensor", None),
        P(), P(), P(None, None, "tensor"), P(None, "tensor", None), P(),
    )
    shards = make_shards(mesh.shape["dp"] // GROUP)
    return jax.shard_map(shards, mesh=mesh, in_specs=in_specs, out_specs=out_specs, check_vma=False)
```

time: 839 us -> 200 us (0.24)
  waiting for transfers between devices: 607 us -> 0 us
  Pallas kernels: 0 us -> 194 us
  matrix products: 122 us -> 0 us
  local copies, waits for them, and re-layouts: 56.4 us -> 4.52 us
  other arithmetic: 33.4 us -> 0 us
  between operations: 15.3 us -> 0.67 us
    psum x4 -> x0, waiting for transfers between devices: 539 us -> none  [the longest x1 206 us: shards(): sum_second, sum_lift_fc1 = lax.psum((part_second, part_lift_fc1), 'tensor')]
    pallas_call x0 -> x2, Pallas kernels: none -> 194 us  [the longest x1 191 us: shards(): pl.pallas_call(lambda *refs: kernel(names, sizes, *refs), out_shape=tuple...]
    dot_general x38 -> x0, matrix products: 122 us -> none  [the longest x12 52.7 us: product(): return jnp.dot(left, right, preferred_element_type=jnp.float32)]
    reduce_scatter x2 -> x0, waiting for transfers between devices: 67.5 us -> none  [the longest x1 51 us: shards(): lax.psum_scatter(own_part.astype(jnp.bfloat16), 'tensor', scatter_dimensi...]
    unnamed x136 -> x8, local copies, waits for them, and re-layouts: 32.1 us -> 4.52 us
    convert_element_type x11 -> x0, other arithmetic: 14.5 us -> none  [the longest x1 4.75 us: shards(): grad_scores = (soft_again * (grad_soft - weighted)).astype(jnp.bfloat16)]
    reduce_sum x6 -> x0, other arithmetic: 14.1 us -> none  [the longest x3 8.97 us: norm_rows(): centred = values - jnp.mean(values, axis=-1, keepdims=True)]
    reshape x5 -> x0, local copies, waits for them, and re-layouts: 9.33 us -> none  [the longest x1 6.69 us: shards(): projected = projected.reshape(seq_count, slot_count, 3, heads_here, HD)]
  transfers between devices with their start and end apart: 7 -> 0, of which waited for: 6 -> 0; matrix products, arithmetic and copies ran while one was open for 15% -> 0% of each run, Pallas kernels for 0% -> 0%
where the time goes in v1:
time: 200 us; the launch traced here: 199 us
  Pallas kernels  194 us (97%)
  local copies, waits for them, and re-layouts  4.52 us (2%)
    pallas_call x1, Pallas kernels, shards(): pl.pallas_call(lambda *refs: kernel(names, sizes, *refs), out_shape=tuple...  191 us
    unnamed x8, local copies, waits for them, and re-layouts  4.52 us

profile of v1, /device:TPU:0, one launch (start us, length us, event | category | flops | bytes accessed | tf_op | source)
XLA Modules:
  0.0 199.4 jit_solution(9725608439358387228)
XLA Ops:
  0.6 191.3 %shard_map.231 = (bf16[4,320,256]{2,1,0:T(8,128)(2,1)}, bf16[4,320,256]{2,1,0:T(8,128)(2,1)}, bf16[8,16,3072]{2,1,0:T(8,128)(2,1)}, bf16[8,4,16,1024]{3,2,1,0:T(8,128)(2,1)}) custom-call(s32[4]{0:T(128)} %refs_0_.1, s32[4,4]{1,0:T(4,128)} %refs_1_.1, bf16[4,320,1024]{2,1,0:T(8,128)(2,1)} %refs_2_.1, bf16[4,320,256]{2,1,0:T(8,128)(2,1)} %refs_3_.1, ...), custom_call_target="tpu_custom_call" | custom-call | tf_op jit(solution)/shard_map/pallas_call | solution.py:648
  192.0 0.0 copy-start
  192.0 1.2 copy-done
  193.2 0.0 copy-start.1
  193.2 1.1 copy-done.1
  194.3 0.0 copy-start.2
  194.3 1.1 copy-done.2
  195.4 0.0 copy-start.3
  195.4 1.1 copy-done.3
  196.5 2.9 %shard_map.232 = (f32[4,320,256]{2,1,0:T(8,128)}, f32[4,320,256]{2,1,0:T(8,128)}, f32[8,16,1024]{2,1,0:T(8,128)}, f32[8,3,16,256]{3,2,1,0:T(8,128)}, f32[8,16,25...) custom-call(bf16[4,320,256]{2,1,0:T(8,128)(2,1)S(1)} %copy-done.2, ...), custom_call_target="tpu_custom_call" | custom-call | tf_op jit(solution)/shard_map/pallas_call | solution.py:664
Async XLA Ops:
  192.0 1.2 copy-start
  193.2 1.1 copy-start.1
  194.3 1.1 copy-start.2
  195.4 1.1 copy-start.3

commit v2 on v1

v2 whole, which is shorter than its diff:
```python
import jax
import jax.numpy as jnp
from jax import lax
from jax.experimental import pallas as pl
from jax.experimental.pallas import tpu as pltpu
from jax.sharding import PartitionSpec as P


BF = jnp.bfloat16
F32 = jnp.float32
MESH = pl.DeviceIdType.MESH
EPSILON = 1e-6
NEG_FILL = -1e30
HD = 64
GROUP = 8
BLOCK = 160
SMALL = 32
STEP = 512


def dot(a, b):
    return lax.dot_general(a, b, (((1,), (0,)), ((), ())), preferred_element_type=F32)


def dot_nt(a, b):
    return lax.dot_general(a, b, (((1,), (1,)), ((), ())), preferred_element_type=F32)


def dot_tn(a, b):
    return lax.dot_general(a, b, (((0,), (0,)), ((), ())), preferred_element_type=F32)


def rows_loop(count, body, block=BLOCK):
    @pl.loop(0, count // block)
    def _(i):
        body(pl.ds(pl.multiple_of(i * block, block), block))


def moments(values):
    centred = values - jnp.mean(values, axis=-1, keepdims=True)
    inverse = lax.rsqrt(jnp.mean(centred * centred, axis=-1, keepdims=True) + EPSILON)
    return centred, inverse


def norm_back(values, grad):
    centred, inverse = moments(values)
    hat = centred * inverse
    return inverse * (
        grad - jnp.mean(grad, axis=-1, keepdims=True) - hat * jnp.mean(grad * hat, axis=-1, keepdims=True)
    )


class Bag:
    pass


def prep(r):
    def body(rows):
        centred, inverse = moments(r.x[rows, :].astype(F32))
        r.first[rows, :] = (centred * inverse).astype(BF)

    rows_loop(r.S, body)


def prep_dz(r):
    def body(rows):
        keep = (lax.broadcasted_iota(jnp.int32, (BLOCK, 1), 0) + rows.start) < r.length
        for j in range(4):
            v = r.dzq[j, rows, :]
            r.dz[rows, r.W * j : r.W * (j + 1)] = jnp.where(keep, v, jnp.zeros_like(v))

    rows_loop(r.S, body)
    r.g_fc2[...] = dot_nt(r.dz[...], r.up_fc2[...]).astype(BF)


def by_head(r, v, ref):
    head = lax.broadcasted_iota(jnp.int32, (r.S, r.W), 1) // HD
    for h in range(r.W // HD):
        ref[h * r.S : (h + 1) * r.S, :] = jnp.where(head == h, v, jnp.zeros_like(v))


def own_lanes(r, t):
    head = lax.broadcasted_iota(jnp.int32, (r.S, r.W), 1) // HD
    out = t[: r.S]
    for h in range(1, r.W // HD):
        out = jnp.where(head == h, t[h * r.S : (h + 1) * r.S], out)
    return out


def block_of(q, width):
    return pl.ds(pl.multiple_of(q * width, width), width)


def attn_fwd(r, q):
    S, W = r.S, r.W
    p = dot(r.first[...], r.wq[q]) + dot(r.lift_qkv[...], r.sel_qu[:, block_of(q, 3 * W)])
    r.proj[q] = p.astype(BF)
    by_head(r, r.proj[q, :, 0:W], r.qm.at[q])
    r.st[...] = dot_nt(r.proj[q, :, W : 2 * W], r.qm[q])
    valid = lax.broadcasted_iota(jnp.int32, (S, 128), 0) < r.length

    for k in range(r.st.shape[1] // 128):
        c = slice(k * 128, (k + 1) * 128)
        v = jnp.where(valid, r.st[:, c] * (HD**-0.5), NEG_FILL)
        e = jnp.exp(v - jnp.max(v, axis=0, keepdims=True))
        soft = e * (1.0 / jnp.sum(e, axis=0, keepdims=True))
        r.soft[q, :, c] = soft
        r.ds[:, c] = soft.astype(BF)

    att = own_lanes(r, dot_tn(r.ds[...], r.proj[q, :, 2 * W : 3 * W])).astype(BF)
    r.att[:, block_of(q, W)] = att
    r.branch[...] += dot(att, r.wo[q])


def after_attn(r):
    r.lift_out[...] = dot_nt(r.att[...], r.sel_od[...]).astype(BF)
    r.branch[...] += dot(r.lift_out[...], r.up_out[...])

    def body(rows):
        mixed = r.x[rows, :].astype(F32) + r.branch[rows, :]
        r.mixed[rows, :] = mixed
        centred, inverse = moments(mixed)
        r.second[rows, :] = (centred * inverse).astype(BF)

    rows_loop(r.S, body)
    r.lift_fc1[...] = dot_nt(r.second[...], r.dn_fc1[...]).astype(BF)
    r.outacc[...] = jnp.zeros_like(r.outacc)
    r.gsec[...] = jnp.zeros_like(r.gsec)
    r.lift_fc2_acc[...] = jnp.zeros_like(r.lift_fc2_acc)
    r.glf1_acc[...] = jnp.zeros_like(r.glf1_acc)


def ffn_unit(r, q, u):
    FQ = r.FQ
    cols = block_of(u, STEP)
    wide = pl.ds(pl.multiple_of(q * FQ + u * STEP, STEP), STEP)
    up1 = r.sel_f1[:, wide]
    dn2 = r.sel_f2[:, wide]
    r.before[...] = dot(r.second[...], r.w1[q, :, cols]) + dot(r.lift_fc1[...], up1)
    r.gh[...] = dot_nt(r.dz[...], r.w2[q, cols, :]) + dot(r.g_fc2[...], dn2)

    def body(rows):
        b = r.before[rows, :]
        cdf = 0.5 * (1.0 + lax.erf(b * (0.5**0.5)))
        r.hidden[rows, :] = (b * cdf).astype(BF)
        slope = cdf + b * jnp.exp(-0.5 * b * b) * 0.3989422804014327
        r.gb[rows, :] = (slope * r.gh[rows, :]).astype(BF)

    for k in range(r.S // SMALL):
        body(pl.ds(k * SMALL, SMALL))
    h = r.hidden[...]
    g = r.gb[...]
    r.outacc[...] += dot(h, r.w2[q, cols, :])
    r.gsec[...] += dot_nt(g, r.w1[q, :, cols])
    r.lift_fc2_acc[...] += dot_nt(h, dn2)
    r.glf1_acc[...] += dot_nt(g, up1)
    r.g_f1[:, wide] = dot_tn(r.lift_fc1[...], g).astype(BF)
    r.g_f2[:, wide] = dot_tn(r.g_fc2[...], h).astype(BF)


def after_ffn_out(r):
    r.outacc[...] += dot(r.lift_fc2[...], r.up_fc2[...])

    def body(rows):
        keep = (lax.broadcasted_iota(jnp.int32, (BLOCK, 1), 0) + rows.start) < r.length
        r.out[rows, :] = jnp.where(keep, r.mixed[rows, :] + r.outacc[rows, :], 0.0).astype(BF)

    rows_loop(r.S, body)


def after_ffn_back(r):
    r.lift_fc2[...] = r.lift_fc2_acc[...].astype(BF)
    g1 = r.glf1_acc[...].astype(BF)
    r.g_f2u[...] = dot_tn(r.lift_fc2[...], r.dz[...]).astype(BF)
    r.g_f1d[...] = dot_tn(g1, r.second[...]).astype(BF)
    r.gsec[...] += dot(g1, r.dn_fc1[...])

    def body(rows):
        g = r.dz[rows, :].astype(F32) + norm_back(r.mixed[rows, :], r.gsec[rows, :])
        r.gsec[rows, :] = g
        r.gbr[rows, :] = g.astype(BF)

    rows_loop(r.S, body)
    gbr = r.gbr[...]
    r.g_ou[...] = dot_tn(r.lift_out[...], gbr).astype(BF)
    r.g_out[...] = dot_nt(gbr, r.up_out[...]).astype(BF)


def back_attended(r):
    W = r.W
    r.ga[...] = dot(r.g_out[...], r.sel_od[...])
    for q in range(4):
        c = slice(q * W, (q + 1) * W)
        r.ga[:, c] += dot_nt(r.gbr[...], r.wo[q])
    r.g_od[...] = dot_tn(r.g_out[...], r.att[...]).astype(BF)


def attn_back(r, q):
    W = r.W
    sc = HD**-0.5
    by_head(r, r.ga[:, block_of(q, W)].astype(BF), r.gm)
    k = r.proj[q, :, W : 2 * W]
    r.st[...] = dot_nt(r.proj[q, :, 2 * W : 3 * W], r.gm[...])
    gv = dot(r.soft[q].astype(BF), r.gm[...])

    for i in range(r.st.shape[1] // 128):
        c = slice(i * 128, (i + 1) * 128)
        soft, gs = r.soft[q, :, c], r.st[:, c]
        r.ds[:, c] = (soft * (gs - jnp.sum(soft * gs, axis=0, keepdims=True))).astype(BF)

    ds = r.ds[...]
    base = pl.multiple_of(3 * W * q, 128)
    r.gp[:, pl.ds(base, W)] = (own_lanes(r, dot_tn(ds, k)) * sc).astype(BF)
    r.gp[:, pl.ds(base + W, W)] = (dot(ds, r.qm[q]) * sc).astype(BF)
    r.gp[:, pl.ds(base + 2 * W, W)] = gv.astype(BF)
    wide = block_of(q, 3 * W)
    r.g_qu[:, wide] = dot_tn(r.lift_qkv[...], r.gp[:, wide]).astype(BF)


def finish_grads(r):
    gq = dot_nt(r.gp[...], r.sel_qu[...]).astype(BF)
    r.g_qd[...] = dot_tn(gq, r.first[...]).astype(BF)
    r.g_qkv[...] = gq


def back_first(r):
    W = r.W
    r.mixed[...] = dot(r.g_qkv[...], r.dn_qkv[...])
    for q in range(4):
        r.mixed[...] += dot_nt(r.gp[:, 3 * W * q : 3 * W * (q + 1)], r.wq[q])


def finish_rows(r, k):
    rows = slice(k * (r.S // 2), (k + 1) * (r.S // 2))
    r.gin[rows, :] = (r.gsec[rows, :] + norm_back(r.x[rows, :].astype(F32), r.mixed[rows, :])).astype(BF)


class Stream:
    def __init__(self, r):
        self.r = r
        d = self.d = lax.axis_index("dp")
        self.z = lax.axis_index("tensor")
        m = self.m = d % GROUP
        self.base = d - m
        self.dx = d + 2 - 4 * ((m // 2) % 2)
        self.dy = d + 4 - 8 * (m // 4)
        self.ds = d + 1 - 2 * (m % 2)
        self.dd = self.dx + self.dy - d
        self.inner = (self.z + 1) // 2 == 1
        self.n_a, self.n = 6, 18

    def quarter(self, i):
        return (self.z + jnp.where(self.z < 2, i, 4 - i)) % 4

    def unit(self, t, f):
        pl.when(t < self.n_a)(lambda: f("A", t % 2, t // 2 + 1))
        pl.when(t >= self.n_a)(lambda: f("B", (t - self.n_a) % 4, (t - self.n_a) // 4 + 1))

    def greet(self):
        bar = pltpu.get_barrier_semaphore()
        for k in range(1, GROUP):
            peer = self.base + (self.m + k) % GROUP
            pl.semaphore_signal(bar, inc=1, device_id=(peer, self.z), device_id_type=MESH)
        for k in range(1, 4):
            pl.semaphore_signal(bar, inc=1, device_id=(self.d, (self.z + k) % 4), device_id_type=MESH)

    def met(self):
        pl.semaphore_wait(pltpu.get_barrier_semaphore(), GROUP + 2)

    def parts(self, kind, p, q, d, half=None):
        r, m = self.r, d - self.base
        first, c = (0, pl.ds(0, r.D)) if half is None else (half, pl.ds(r.D // 2 * half, r.D // 2))
        if kind == "A":
            n = r.D // GROUP // 2
            k = r.W // GROUP // 2
            part = n if half is None else n // 2
            a = pl.ds(pl.multiple_of((2 * m + p) * n + first * part, part), part)
            b = pl.ds(pl.multiple_of((2 * m + p) * k, k), k)
            return ((r.wq.at[q, a, :]), (r.wo.at[q, b, c]))
        n = r.D // GROUP
        width = r.FQ // 4
        k = width // GROUP
        part = n if half is None else n // 2
        a = pl.ds(pl.multiple_of(m * n + first * part, part), part)
        b = pl.ds(pl.multiple_of(p * width + m * k, k), k)
        return (r.w1.at[q, a, block_of(p, width)], r.w2.at[q, b, c])

    def own(self, kind, p):
        r, m, z = self.r, self.m, self.z
        first, second = self.parts(kind, p, z, self.d)
        if kind == "A":
            n = r.D // GROUP // 2
            k = r.W // GROUP // 2
            a = pl.ds(pl.multiple_of((2 * m + p) * n, n), n)
            pairs = [(r.hq.at[i, a, :], r.wq.at[z, a, pl.ds(i * r.W, r.W)]) for i in range(3)]
            return pairs + [(r.ho.at[pl.ds(pl.multiple_of((2 * m + p) * k, k), k), :], second)]
        n = r.D // GROUP
        k = r.FQ // 4 // GROUP
        a = pl.ds(pl.multiple_of(m * n, n), n)
        b = pl.ds(pl.multiple_of(p * (r.FQ // 4) + m * k, k), k)
        return [(r.h1.at[a, block_of(p, r.FQ // 4)], first), (r.h2.at[b, :], second)]

    def send(self, srcs, dsts, sem, dev):
        for s, t in zip(srcs, dsts):
            pltpu.make_async_remote_copy(
                src_ref=s, dst_ref=t, send_sem=self.r.sends, recv_sem=sem, device_id=dev, device_id_type=MESH
            ).start()

    def wait(self, rows, sem):
        v = self.r.w2.at[0, pl.ds(0, rows), :]
        pltpu.make_async_copy(v, v, sem).wait()

    def index(self, kind, p, i):
        return (i - 1) * 2 + p if kind == "A" else 6 + (i - 1) * 4 + p

    def inner_sends(self, kind, p):
        z, d = self.z, self.d

        @pl.when(self.inner)
        def _():
            src, dst = zip(*self.own(kind, p))
            for to in (3 * (z - 1), 3 - z):
                self.send(src, dst, self.r.rz.at[self.index(kind, p, 1)], (d, to))

    def outer_sends(self, kind, p, i):
        z, d = self.z, self.d

        @pl.when(z % 3 == 0)
        def _():
            src, dst = zip(*self.own(kind, p))
            to = 2 - z // 3 if i == 2 else 1 + z // 3
            self.send(src, dst, self.r.rz.at[self.index(kind, p, i)], (d, to))

    def z_stage(self, t):
        self.wait(64, self.r.rz.at[t])

        def forward(kind, p, i):
            @pl.when(self.inner & (i < 3))
            def _():
                piece = self.parts(kind, p, self.quarter(i), self.d)
                self.send(piece, piece, self.r.rz.at[self.index(kind, p, i + 1)], (self.d, 3 * (self.z - 1)))

        self.unit(t, forward)

    def xy_sends(self, t):
        def go(kind, p, i):
            z, r = self.z, self.r
            piece = self.parts(kind, p, self.quarter(i), self.d)
            self.send(piece, piece, r.rx.at[t], (self.dx, z))
            self.send(piece, piece, r.ry.at[t], (self.dy, z))
            self.send(piece, piece, r.rs.at[t], (self.ds, z))

        self.unit(t, go)

    def xy_stage(self, t):
        def go(kind, p, i):
            z, q, r = self.z, self.quarter(i), self.r
            for sem, frm, to, half in ((r.rx, self.dx, self.dy, 0), (r.ry, self.dy, self.dx, 1)):
                self.wait(64, sem.at[t])
                h = self.parts(kind, p, q, frm, half)
                self.send(h, h, r.rd.at[t], (to, z))
                w = self.parts(kind, p, q, frm)
                self.send(w, w, r.rs.at[t], (self.ds, z))

        self.unit(t, go)

    def d_stage(self, t):
        def go(kind, p, i):
            self.wait(64, self.r.rd.at[t])
            w = self.parts(kind, p, self.quarter(i), self.dd)
            self.send(w, w, self.r.rs.at[t], (self.ds, self.z))

        self.unit(t, go)

    def s_stage(self, t):
        self.wait(256, self.r.rs.at[t])

    def finish_sends(self):
        kinds = 6
        always = 7 * self.n + 2 * kinds

        @pl.loop(0, jnp.where(self.inner, always + 2 * kinds, always))
        def _(i):
            self.wait(64, self.r.sends)


    def to_planes(self, view, target, send_sem, recv_sem):
        for k in range(1, 4):
            j = (self.z + k) % 4
            pltpu.make_async_remote_copy(
                src_ref=view(j), dst_ref=target, send_sem=send_sem, recv_sem=recv_sem, device_id=(self.d, j), device_id_type=MESH
            ).start()

    def to_group(self, view, target, send_sem, recv_sem):
        for k in range(1, GROUP):
            m = (self.m + k) % GROUP
            pltpu.make_async_remote_copy(
                src_ref=view(m), dst_ref=target, send_sem=send_sem, recv_sem=recv_sem, device_id=(self.base + m, self.z), device_id_type=MESH
            ).start()

    def share(self, src, dst, sems):
        place = dst(self.m)
        for to in (self.dx, self.dy, self.dd):
            pltpu.make_async_remote_copy(
                src_ref=src, dst_ref=place, send_sem=sems[0], recv_sem=sems[1], device_id=(to, self.z), device_id_type=MESH
            ).start()
        pltpu.make_async_remote_copy(
            src_ref=src, dst_ref=place, send_sem=sems[2], recv_sem=sems[3], device_id=(self.ds, self.z), device_id_type=MESH
        ).start()

    def pass_on(self, three, dst, sems):
        self.done(three, sems[1])
        for frm in (self.dx, self.dy, self.dd):
            place = dst(frm - self.base)
            pltpu.make_async_remote_copy(
                src_ref=place, dst_ref=place, send_sem=sems[2], recv_sem=sems[3], device_id=(self.ds, self.z), device_id_type=MESH
            ).start()

    def done(self, ref, *sems):
        for s in sems:
            pltpu.make_async_copy(ref, ref, s).wait()


class Sems:
    def __init__(self, ref, first):
        self.ref, self.first = ref, first

    def __getitem__(self, k):
        if isinstance(k, slice):
            return [self[i] for i in range(k.start, k.stop)]
        return self.ref.at[self.first + k]


def one_hot(r, p, transposed):
    R, T, n = r.R, r.T, r.n_img
    shape = (T, n * R) if transposed else (n * R, T)
    a = lax.broadcasted_iota(jnp.int32, shape, 1 if transposed else 0)
    b = lax.broadcasted_iota(jnp.int32, shape, 0 if transposed else 1)
    owner = jnp.zeros(shape, jnp.int32)
    for i in range(n):
        owner = jnp.where(a // R == i, r.ids[i, p], owner)
    hit = (b // R == owner) & (a % R == b % R)
    return jnp.where(hit, 1.0, 0.0).astype(BF)


def choose(r, p, flat):
    shape = (r.R, r.T)
    a = lax.broadcasted_iota(jnp.int32, shape, 0)
    b = lax.broadcasted_iota(jnp.int32, shape, 1)
    hit = (b // r.R == r.my_ids[p]) & (a == b % r.R)
    return dot(jnp.where(hit, 1.0, 0.0).astype(BF), flat).astype(BF)


def kernel(names, sizes, *refs):
    r = Bag()
    for n, f in zip(names, refs):
        setattr(r, n, f)
    for n, v in sizes.items():
        setattr(r, n, v)
    c = Stream(r)
    z, d = c.z, c.d
    S, W, FQ, R, n = r.S, r.W, r.FQ, r.R, r.n_img
    r.before, r.gh = r.st.at[:, pl.ds(0, STEP)], r.st.at[:, pl.ds(STEP, STEP)]
    r.hidden, r.gb = r.ds.at[:, pl.ds(0, STEP)], r.ds.at[:, pl.ds(STEP, STEP)]
    r.ga = r.branch
    r.out, r.gin = r.second, r.first
    r.length = r.len[z]
    r.my_ids = [r.ids[z, p] for p in range(4)]
    c.greet()
    load = []

    def fetch(ends):
        slot = len(load)
        copy = lambda: pltpu.make_async_copy(*ends(), r.loc.at[slot])
        copy().start()
        load.append(copy)
        return copy

    l_x = fetch(lambda: (r.tokens.at[z], r.x))
    l_ad = {k: fetch(lambda k=k: (getattr(r, "h_" + k), getattr(r, k))) for k in ("aqd", "aqu", "aod", "a1u", "a2d", "aou", "a1d", "a2u")}
    l_q = [fetch(lambda i=i: (r.hq.at[i], r.wq.at[z, :, pl.ds(i * W, W)])) for i in range(3)]
    l_q.append(fetch(lambda: (r.ho, r.wo.at[z])))
    l_f = [fetch(lambda: (r.h1, r.w1.at[z])), fetch(lambda: (r.h2, r.w2.at[z]))]
    l_c = fetch(lambda: (r.cot.at[z], r.dzq.at[z]))
    c.met()

    def wait_all(copies):
        for copy in copies:
            copy().wait()

    def pick_attn():
        wait_all([l_ad["aqu"], l_ad["aod"]])
        hot = one_hot(r, 0, False)
        for i in range(3):
            r.out_qu[:, :, i * W : (i + 1) * W] = dot(hot, r.aqu[:, i].reshape(r.T, W)).astype(BF).reshape(n, R, W)
        r.out_od[...] = dot(one_hot(r, 1, False), r.aod[...]).astype(BF).reshape(n, R, W)
        c.to_planes(lambda j: r.out_qu.at[j], r.sel_qu.at[:, block_of(z, 3 * W)], r.misc.at[0], r.misc.at[1])
        c.to_planes(lambda j: r.out_od.at[j], r.sel_od.at[:, block_of(z, W)], r.misc.at[70], r.misc.at[71])
        r.sel_qu[:, block_of(z, 3 * W)] = r.out_qu[z]
        r.sel_od[:, block_of(z, W)] = r.out_od[z]

    def have_attn():
        c.done(r.sel_qu.at[:, pl.ds(0, 9 * W)], r.misc.at[0], r.misc.at[1])
        c.done(r.sel_od.at[:, pl.ds(0, 3 * W)], r.misc.at[70], r.misc.at[71])

    def pick_ffn():
        wait_all([l_ad["a1u"], l_ad["a2d"]])
        r.out_f1[...] = dot(one_hot(r, 2, False), r.a1u[...]).astype(BF).reshape(n, R, FQ)
        r.out_f2[...] = dot(one_hot(r, 3, False), r.a2d[...]).astype(BF).reshape(n, R, FQ)
        r.sel_f1[:, block_of(z, FQ)] = r.out_f1[z]
        r.sel_f2[:, block_of(z, FQ)] = r.out_f2[z]

    def send_f1():
        c.to_planes(lambda j: r.out_f1.at[j], r.sel_f1.at[:, block_of(z, FQ)], r.misc.at[72], r.misc.at[73])

    def send_f2():
        c.to_planes(lambda j: r.out_f2.at[j], r.sel_f2.at[:, block_of(z, FQ)], r.misc.at[74], r.misc.at[75])

    def have_ffn():
        c.done(r.sel_f1.at[:, pl.ds(0, 3 * FQ)], r.misc.at[72], r.misc.at[73])
        c.done(r.sel_f2.at[:, pl.ds(0, 3 * FQ)], r.misc.at[74], r.misc.at[75])

    def pick_first():
        l_ad["aqd"]().wait()
        r.dn_qkv[...] = choose(r, 0, r.aqd[...])
        r.lift_qkv[...] = dot_nt(r.first[...], r.dn_qkv[...]).astype(BF)

    def pick_rest():
        wait_all([l_ad["aou"], l_ad["a1d"], l_ad["a2u"]])
        r.up_out[...] = choose(r, 1, r.aou[...])
        r.dn_fc1[...] = choose(r, 2, r.a1d[...])
        r.up_fc2[...] = choose(r, 3, r.a2u[...])

    CUTS = 5

    def send_cot(k):
        rows = pl.ds(k * (S // CUTS), S // CUTS)
        c.to_planes(lambda j: r.cot.at[j, rows, :], r.dzq.at[z, rows, :], r.misc.at[2], r.misc.at[3])

    def have_cot():
        c.done(r.dzq.at[pl.ds(0, 3)], r.misc.at[2], r.misc.at[3])
        l_c().wait()
        prep_dz(r)

    def ffn(n):
        i, u = n // 2, n % 2
        q = c.quarter(i)
        ffn_unit(r, q, u)

        @pl.when(i > 0)
        def _():
            wide = pl.ds(pl.multiple_of(q * FQ + u * STEP, STEP), STEP)
            for ref, base in ((r.g_f1, 0), (r.g_f2, FQ)):
                pltpu.make_async_remote_copy(
                    src_ref=ref.at[:, wide], dst_ref=r.sp.at[z, :, pl.ds(pl.multiple_of(base + u * STEP, STEP), STEP)],
                    send_sem=r.misc.at[8], recv_sem=r.misc.at[9], device_id=(d, q), device_id_type=MESH,
                ).start()

    N = c.n
    LZ, LX, LD = 2, 1, 1
    lag = LZ + LX + LD
    c.inner_sends("A", 0)
    c.inner_sends("A", 1)
    l_x().wait()
    prep(r)
    r.branch[...] = jnp.zeros_like(r.branch)
    c.z_stage(0)

    @pl.loop(0, N + lag)
    def _(t):
        pl.when(t < N)(lambda: c.xy_sends(t))
        pl.when((t >= LZ) & (t < LZ + N))(lambda: c.xy_stage(t - LZ))
        pl.when((t >= LZ + LX) & (t < LZ + LX + N))(lambda: c.d_stage(t - LZ - LX))
        pl.when(t >= lag)(lambda: c.s_stage(t - lag))
        pl.when(t + 1 < N)(lambda: c.z_stage(t + 1))
        pl.when(t < 4)(lambda: c.inner_sends("B", t))

        @pl.when((t == 0) | (t == 2))
        def _():
            for p in range(2):
                pl.when(t == 0)(lambda: c.outer_sends("A", p, 2))
                pl.when(t == 2)(lambda: c.outer_sends("A", p, 3))

        pl.when((t >= 2) & (t < 6))(lambda: c.outer_sends("B", t - 2, 2))
        pl.when((t >= 6) & (t < 10))(lambda: c.outer_sends("B", t - 6, 3))
        pl.when((t >= 3) & (t < 3 + 2 * CUTS) & (t % 2 == 1))(lambda: send_cot((t - 3) // 2))
        pl.when(t == 0)(pick_first)
        pl.when(t == 1)(pick_attn)
        pl.when(t == 2)(lambda: wait_all(l_q))
        pl.when(t == 3)(pick_rest)
        pl.when(t == 4)(pick_ffn)
        pl.when(t == 9)(send_f1)
        pl.when(t == 11)(send_f2)
        pl.when(t == 1 + lag)(have_attn)
        pl.when((t == 2) | (t == 1 + lag) | (t == 3 + lag) | (t == 5 + lag))(lambda: attn_fwd(r, c.quarter((t - 2) // 2)))

        @pl.when(t == 5 + lag)
        def _():
            after_attn(r)
            wait_all(l_f)

        pl.when(t == 13)(have_cot)
        pl.when(t == 15)(have_ffn)
        pl.when((t >= 13) & (t != 20))(lambda: ffn(jnp.minimum(t - 13, 7)))

    mine = block_of(z, W)

    def cut(ref):
        return lambda j: ref.at[:, block_of(j, W)]

    def group(lo, own_end, hi, s, fs, fr, out=None):
        cols, own, reps, zc = pl.ds(lo, hi - lo), pl.ds(lo, own_end - lo), pl.ds(own_end, hi - own_end), pl.ds(fr, hi - own_end)
        sem = Sems(r.misc, s)
        fin = pl.ds(fs, own_end - lo)
        fin_s = r.fin_s if out is None else out

        def send_whole(ref, col):
            c.to_planes(lambda j: ref, r.sp.at[z, :, cols], sem[0], sem[1])
            r.sp[z, :, cols] = ref[...]

        def send(sources):
            for ref, width, col in sources:
                c.to_planes(lambda j: ref.at[:, block_of(j, width)], r.sp.at[z, :, pl.ds(col, width)], sem[0], sem[1])
                r.sp[z, :, col : col + width] = ref[:, block_of(z, width)]

        def expand():
            c.done(r.sp.at[pl.ds(0, 3), :, cols], sem[0], sem[1])
            for a, b, p in r.blocks:
                if lo <= a < hi:
                    r.dense[:, a:b] = dot(one_hot(r, p, True), r.sp[:, :, a:b].reshape(n * R, b - a)).astype(BF)
            c.to_group(lambda m: r.dense.at[block_of(m, R), cols], r.rsb.at[c.m, :, cols], sem[2], sem[3])
            r.rsb[c.m, :, cols] = r.dense[block_of(c.m, R), cols]

        def reduce():
            c.done(r.rsb.at[pl.ds(0, GROUP - 1), :, cols], sem[2], sem[3])
            sums = r.rsb[0, :, cols].astype(F32)
            for k in range(1, GROUP):
                sums = sums + r.rsb[k, :, cols].astype(F32)
            r.red[:, cols] = sums.astype(BF)
            if hi > own_end:
                c.to_planes(lambda j: r.red.at[:, reps], r.zb.at[z, :, zc], sem[4], sem[5])
                r.zb[z, :, zc] = r.red[:, reps]
            if own_end > lo:
                c.share(r.red.at[:, own], lambda m: fin_s.at[m, :, fin], sem[6:10])
                fetch(lambda: (r.red.at[:, own], fin_s.at[c.m, :, fin]))

        def share():
            c.done(r.zb.at[pl.ds(0, 3), :, zc], sem[4], sem[5])
            c.share(r.zb.at[:, :, zc], lambda m: r.fin_r.at[m, :, :, zc], sem[10:14])
            fetch(lambda: (r.zb.at[:, :, zc], r.fin_r.at[c.m, :, :, zc]))

        def relay():
            if own_end > lo:
                c.pass_on(fin_s.at[pl.ds(0, 3), :, fin], lambda m: fin_s.at[m, :, fin], sem[6:10])

        def relay_rep():
            c.pass_on(r.fin_r.at[pl.ds(0, 3), :, :, zc], lambda m: r.fin_r.at[m, :, :, zc], sem[10:14])

        def close():
            if own_end > lo:
                c.done(fin_s.at[pl.ds(0, 3), :, fin], sem[6])
                c.done(fin_s.at[pl.ds(0, 4), :, fin], sem[8], sem[9])
            if hi > own_end:
                c.done(r.fin_r.at[pl.ds(0, 3), :, :, zc], sem[10])
                c.done(r.fin_r.at[pl.ds(0, 4), :, :, zc], sem[12], sem[13])

        return send if out is None else send_whole, expand, reduce, share, relay, relay_rep, close

    m0, l0, end = r.starts
    _, e_expand, e_reduce, _, e_relay, _, e_close = group(0, m0, m0, 8, 0, 0)
    m_send, m_expand, m_reduce, m_share, _, m_relay, m_close = group(m0, m0, l0, 22, 0, 0)
    p0 = l0 + 4 * W
    l_send, l_expand, l_reduce, _, l_relay, _, l_close = group(l0, p0, p0, 36, 2 * FQ, 0)
    p_send, p_expand, p_reduce, _, p_relay, _, p_close = group(p0, end, end, 56, 0, 0, r.fin_p)

    def back(q):
        attn_back(r, q)
        for ref, width, col in ((r.g_qu, 3 * W, l0), (r.g_od, W, l0 + 3 * W)):
            src, dst = ref.at[:, block_of(q, width)], r.sp.at[z, :, pl.ds(col, width)]

            @pl.when(z != q)
            def _():
                pltpu.make_async_remote_copy(
                    src_ref=src, dst_ref=dst, send_sem=r.misc.at[36], recv_sem=r.misc.at[37], device_id=(d, q), device_id_type=MESH
                ).start()

    after_ffn_back(r)
    m_send([(r.g_f1d, W, m0), (r.g_f2u, W, m0 + W), (r.g_ou, W, m0 + 2 * W)])
    after_ffn_out(r)
    c.to_planes(cut(r.out), r.outr.at[z], r.misc.at[4], r.misc.at[5])
    fetch(lambda: (r.out.at[:, mine], r.outr.at[z]))
    for ref, base in ((r.g_f1, 0), (r.g_f2, FQ)):
        r.sp[z, :, base : base + FQ] = ref[:, block_of(z, FQ)]
    back_attended(r)
    e_expand()

    @pl.loop(0, 4)
    def _(q):
        back(q)

    e_reduce()
    m_expand()
    finish_grads(r)
    p_send(r.g_qd, p0)
    for ref, width, col in ((r.g_qu, 3 * W, l0), (r.g_od, W, l0 + 3 * W)):
        r.sp[z, :, col : col + width] = ref[:, block_of(z, width)]
    m_reduce()
    back_first(r)
    half = S // 2

    def send_gin(k):
        rows = pl.ds(k * half, half)
        c.to_planes(lambda j: r.gin.at[rows, block_of(j, W)], r.ginr.at[z, rows, :], r.misc.at[6], r.misc.at[7])
        fetch(lambda: (r.gin.at[rows, mine], r.ginr.at[z, rows, :]))

    p_expand()
    l_expand()
    finish_rows(r, 0)
    send_gin(0)
    finish_rows(r, 1)
    send_gin(1)
    e_relay()
    m_share()
    p_reduce()
    l_reduce()
    m_relay()
    l_relay()
    p_relay()
    e_close()
    m_close()
    c.done(r.outr.at[pl.ds(0, 3)], r.misc.at[4], r.misc.at[5])
    c.finish_sends()
    l_close()
    p_close()
    c.done(r.ginr.at[pl.ds(0, 3)], r.misc.at[6], r.misc.at[7])
    wait_all(load[1 + len(l_ad) + 7 :])


def spread(names, *refs):
    r = Bag()
    for n, f in zip(names, refs):
        setattr(r, n, f)
    W = r.b_out.shape[2]
    FQ = r.v_f1u.shape[2]
    loads = []
    for k, (src, dst) in enumerate(((r.outr, r.b_out), (r.ginr, r.b_gin), (r.fin_s, r.b_s), (r.fin_r, r.b_r), (r.fin_p, r.b_p))):
        loads.append(pltpu.make_async_copy(src, dst, r.sem_in.at[k]))
        loads[-1].start()
    stores = []

    def store(key):
        stores.append(pltpu.make_async_copy(getattr(r, "v_" + key), getattr(r, "o_" + key), r.sem_out.at[len(stores)]))
        stores[-1].start()

    def widen(ref, value):
        ref[...] = value.astype(F32)

    loads[0].wait()
    widen(r.v_out, r.b_out[...])
    store("out")
    loads[1].wait()
    widen(r.v_gin, r.b_gin[...])
    store("gin")
    loads[2].wait()
    widen(r.v_f1u, r.b_s[:, :, :FQ])
    store("f1u")
    widen(r.v_f2d, r.b_s[:, :, FQ : 2 * FQ])
    store("f2d")
    for i in range(3):
        r.v_qu[:, i] = r.b_s[:, :, 2 * FQ + i * W : 2 * FQ + (i + 1) * W].astype(F32)
    store("qu")
    widen(r.v_od, r.b_s[:, :, 2 * FQ + 3 * W :])
    store("od")
    loads[3].wait()
    for k, key in enumerate(("f1d", "f2u", "ou")):
        for j in range(4):
            getattr(r, "v_" + key)[:, :, W * j : W * (j + 1)] = r.b_r[:, j, :, W * k : W * (k + 1)].astype(F32)
        store(key)
    loads[4].wait()
    widen(r.v_qd, r.b_p[...])
    store("qd")
    for cp in stores:
        cp.wait()


def make_shards(groups):
    def shards(
        tokens, lengths, adapter_ids, qkv_weight, qkv_down, qkv_up, out_weight, out_down, out_up,
        fc1_weight, fc1_down, fc1_up, fc2_weight, fc2_down, fc2_up, cotangent,
    ):
        n, S, D = tokens.shape
        A, _, R = qkv_down.shape
        T = A * R
        W = out_weight.shape[0]
        FQ = fc1_weight.shape[1]
        m0 = 2 * FQ
        l0 = m0 + 3 * W
        total = l0 + 4 * W + D
        blocks = (
            (0, FQ, 2), (FQ, m0, 3), (m0, m0 + W, 2), (m0 + W, m0 + 2 * W, 3), (m0 + 2 * W, l0, 1),
            (l0, l0 + 3 * W, 0), (l0 + 3 * W, l0 + 4 * W, 1), (l0 + 4 * W, total, 0),
        )
        sizes = dict(n_img=n, S=S, D=D, R=R, T=T, W=W, FQ=FQ, starts=(m0, l0, total), blocks=blocks)

        def turned(a):
            return jnp.transpose(a, (0, 2, 1)).reshape(T, a.shape[1])

        args = dict(
            len=lengths, ids=adapter_ids, tokens=tokens, cot=cotangent,
            hq=jnp.transpose(qkv_weight, (1, 0, 2)), ho=out_weight, h1=fc1_weight, h2=fc2_weight,
            h_aqd=turned(qkv_down), h_aqu=jnp.transpose(qkv_up, (0, 2, 1, 3)), h_aod=turned(out_down),
            h_a1u=fc1_up.reshape(T, FQ), h_a2d=turned(fc2_down), h_aou=out_up.reshape(T, D),
            h_a1d=turned(fc1_down), h_a2u=fc2_up.reshape(T, D),
        )
        outs = dict(outr=(n, S, W), ginr=(n, S, W), fin_s=(GROUP, R, 2 * FQ + 4 * W), fin_r=(GROUP, 4, R, 3 * W), fin_p=(GROUP, R, D))
        heads = W // HD
        vm = dict(
            wq=((4, D, 3 * W), BF), wo=((4, W, D), BF), w1=((4, D, FQ), BF), w2=((4, FQ, D), BF),
            aqd=((T, D), BF), aqu=((A, 3, R, W), BF), aod=((T, W), BF), a1u=((T, FQ), BF), a2d=((T, FQ), BF),
            aou=((T, D), BF), a1d=((T, D), BF), a2u=((T, D), BF),
            out_qu=((n, R, 3 * W), BF), out_od=((n, R, W), BF), out_f1=((n, R, FQ), BF), out_f2=((n, R, FQ), BF),
            sel_qu=((R, 12 * W), BF), sel_od=((R, 4 * W), BF), sel_f1=((R, 4 * FQ), BF), sel_f2=((R, 4 * FQ), BF),
            dn_qkv=((R, D), BF), up_out=((R, D), BF), dn_fc1=((R, D), BF), up_fc2=((R, D), BF),
            x=((S, D), BF), dzq=((4, S, W), BF), dz=((S, D), BF),
            first=((S, D), BF), lift_qkv=((S, R), BF), g_fc2=((S, R), BF), proj=((4, S, 3 * W), BF), qm=((4, heads * S, W), BF),
            st=((S, heads * S), F32), ds=((S, heads * S), BF), soft=((4, S, heads * S), F32), att=((S, 4 * W), BF),
            branch=((S, D), F32), lift_out=((S, R), BF), mixed=((S, D), F32), second=((S, D), BF), lift_fc1=((S, R), BF),
            outacc=((S, D), F32), gsec=((S, D), F32), lift_fc2_acc=((S, R), F32), glf1_acc=((S, R), F32),
            lift_fc2=((S, R), BF), gbr=((S, D), BF), g_out=((S, R), BF), gm=((heads * S, W), BF), gp=((S, 12 * W), BF),
            g_qkv=((S, R), BF),
            g_f1=((R, 4 * FQ), BF), g_f2=((R, 4 * FQ), BF), g_f1d=((R, D), BF), g_f2u=((R, D), BF), g_ou=((R, D), BF),
            g_qu=((R, 12 * W), BF), g_od=((R, 4 * W), BF), g_qd=((R, D), BF),
            sp=((n, R, total), BF), dense=((T, total), BF), rsb=((GROUP, R, total), BF), red=((R, total), BF),
            zb=((4, R, 3 * W), BF),
        )
        units = 18
        sems = dict(rz=units, rx=units, ry=units, rd=units, rs=units, sends=None, loc=28, misc=76)
        names = list(args) + list(outs) + list(vm) + list(sems)
        anywhere = pl.BlockSpec(memory_space=pl.ANY)
        got = pl.pallas_call(
            lambda *refs: kernel(names, sizes, *refs),
            out_shape=tuple(jax.ShapeDtypeStruct(s, BF) for s in outs.values()),
            in_specs=[pl.BlockSpec(memory_space=pltpu.SMEM)] * 2 + [anywhere] * (len(args) - 2),
            out_specs=tuple([anywhere] * len(outs)),
            scratch_shapes=[pltpu.VMEM(s, t) for s, t in vm.values()]
            + [pltpu.SemaphoreType.DMA if k is None else pltpu.SemaphoreType.DMA((k,)) for k in sems.values()],
            compiler_params=pltpu.CompilerParams(collective_id=0, has_side_effects=True, vmem_limit_bytes=60 * 2**20),
        )(*args.values())
        outr, ginr, fin_s, fin_r, fin_p = got
        if groups > 1:
            across = [[m + GROUP * g for g in range(groups)] for m in range(GROUP)]
            fin_s, fin_r, fin_p = lax.psum(tuple(v.astype(F32) for v in (fin_s, fin_r, fin_p)), "dp", axis_index_groups=across)
        full = (A, R, D)
        wide = dict(
            out=(n, S, W), gin=(n, S, W), qd=full, qu=(A, 3, R, W), od=(A, R, W), ou=full, f1d=full, f1u=(A, R, FQ), f2d=(A, R, FQ), f2u=full
        )
        held = dict(b_out=outr, b_gin=ginr, b_s=fin_s, b_r=fin_r, b_p=fin_p)
        names = ["outr", "ginr", "fin_s", "fin_r", "fin_p"] + ["o_" + k for k in wide] + list(held) + ["v_" + k for k in wide] + ["sem_in", "sem_out"]
        output, input_grad, qd, qu, od, ou, f1d, f1u, f2d, f2u = pl.pallas_call(
            lambda *refs: spread(names, *refs),
            out_shape=tuple(jax.ShapeDtypeStruct(v, F32) for v in wide.values()),
            in_specs=[anywhere] * 5,
            out_specs=tuple([anywhere] * len(wide)),
            scratch_shapes=[pltpu.VMEM(v.shape, v.dtype) for v in held.values()]
            + [pltpu.VMEM(v, F32) for v in wide.values()]
            + [pltpu.SemaphoreType.DMA((5,)), pltpu.SemaphoreType.DMA((len(wide),))],
            compiler_params=pltpu.CompilerParams(vmem_limit_bytes=60 * 2**20),
        )(outr, ginr, fin_s, fin_r, fin_p)
        back = lambda a: jnp.transpose(a, (0, 2, 1))
        return (output, input_grad, back(qd), jnp.transpose(qu, (0, 2, 1, 3)), back(od), ou, back(f1d), f1u, back(f2d), f2u)

    return shards


def solution(mesh):
    in_specs = (
        P("dp", None, None), P("dp"), P("dp", None), P(None, None, "tensor"), P(), P(None, None, None, "tensor"),
        P("tensor", None), P(None, "tensor", None), P(), P(None, "tensor"), P(), P(None, None, "tensor"),
        P("tensor", None), P(None, "tensor", None), P(), P("dp", None, "tensor"),
    )
    out_specs = (
        P("dp", None, "tensor"), P("dp", None, "tensor"), P(), P(None, None, None, "tensor"), P(None, "tensor", None),
        P(), P(), P(None, None, "tensor"), P(None, "tensor", None), P(),
    )
    shards = make_shards(mesh.shape["dp"] // GROUP)
    return jax.shard_map(shards, mesh=mesh, in_specs=in_specs, out_specs=out_specs, check_vma=False)
```

time: 200 us -> 153 us (0.77)
  Pallas kernels: 194 us -> 152 us
  local copies, waits for them, and re-layouts: 4.52 us -> 0 us
    pallas_call x1, Pallas kernels: 191 us -> 148 us  [shards(): pl.pallas_call(lambda *refs: kernel(names, sizes, *refs), out_shape=tuple...]
    unnamed x8 -> x0, local copies, waits for them, and re-layouts: 4.52 us -> none
where the time goes in v2:
time: 153 us; the launch traced here: 152 us
  Pallas kernels  152 us (99%)
    pallas_call x1, Pallas kernels, shards(): pl.pallas_call(lambda *refs: kernel(names, sizes, *refs), out_shape=tuple...  148 us
    pallas_call x1, Pallas kernels, shards(): pl.pallas_call(lambda *refs: spread(names, *refs), out_shape=tuple((jax.S...  3.95 us

profile of v2, /device:TPU:0, one launch (start us, length us, event | category | flops | bytes accessed | tf_op | source)
XLA Modules:
  0.0 152.5 jit_solution(8769513366782064395)
XLA Ops:
  0.6 147.7 %shard_map.231 = (bf16[4,320,256]{2,1,0:T(8,128)(2,1)}, bf16[4,320,256]{2,1,0:T(8,128)(2,1)}, bf16[8,16,3072]{2,1,0:T(8,128)(2,1)}, bf16[8,4,16,768]{3,2,1,0:T(8,128)(2,1)}, bf16[8,16,1024]{2,1,0:T(8,128)(2,1)}) custom-call(s32[4]{0:T(128)} %refs_0_.1, s32[4,4]{1,0:T(4,128)} %refs_1_.1, bf16[4,320,1024]{2,1,0:T(8,128)(2,1)} %refs_2_.1, ...), custom_call_target="tpu_custom_call" | custom-call | tf_op jit(solution)/shard_map/pallas_call | solution.py:840
  148.3 4.0 %shard_map.232 = (f32[4,320,256]{2,1,0:T(8,128)}, f32[4,320,256]{2,1,0:T(8,128)}, f32[8,16,1024]{2,1,0:T(8,128)}, f32[8,3,16,256]{3,2,1,0:T(8,128)}, f32[8,16,25...) custom-call(bf16[4,320,256]{2,1,0:T(8,128)(2,1)} %get-tuple-element., ...), custom_call_target="tpu_custom_call" | custom-call | tf_op jit(solution)/shard_map/pallas_call | solution.py:859

commit v3 on v2

--- a/solution.py
+++ b/solution.py
@@ -163,13 +163,14 @@
 
     def body(rows):
         keep = (lax.broadcasted_iota(jnp.int32, (BLOCK, 1), 0) + rows.start) < r.length
-        r.out[rows, :] = jnp.where(keep, r.mixed[rows, :] + r.outacc[rows, :], 0.0).astype(BF)
+        v = jnp.where(keep, r.mixed[rows, :] + r.outacc[rows, :], 0.0).astype(BF)
+        for j in range(4):
+            r.outq[j, rows, :] = v[:, r.W * j : r.W * (j + 1)]
 
     rows_loop(r.S, body)
 
 
 def after_ffn_back(r):
-    r.lift_fc2[...] = r.lift_fc2_acc[...].astype(BF)
     g1 = r.glf1_acc[...].astype(BF)
     r.g_f2u[...] = dot_tn(r.lift_fc2[...], r.dz[...]).astype(BF)
     r.g_f1d[...] = dot_tn(g1, r.second[...]).astype(BF)
@@ -254,7 +255,13 @@
 
     def unit(self, t, f):
         pl.when(t < self.n_a)(lambda: f("A", t % 2, t // 2 + 1))
-        pl.when(t >= self.n_a)(lambda: f("B", (t - self.n_a) % 4, (t - self.n_a) // 4 + 1))
+        pl.when((t >= self.n_a) & (t < self.n - 4))(lambda: f("B", (t - self.n_a) % 4, (t - self.n_a) // 4 + 1))
+        last = t - (self.n - 4)
+        pl.when((last >= 0) & (last % 2 == 0))(lambda: f("X", last, 3))
+        pl.when((last >= 0) & (last % 2 == 1))(lambda: f("Y", last, 3))
+
+    def pair(self, kind):
+        return (self.dy, self.dx) if kind == "X" else (self.dx, self.dy)
 
     def greet(self):
         bar = pltpu.get_barrier_semaphore()
@@ -285,9 +292,11 @@
         b = pl.ds(pl.multiple_of(p * width + m * k, k), k)
         return (r.w1.at[q, a, block_of(p, width)], r.w2.at[q, b, c])
 
-    def own(self, kind, p):
-        r, m, z = self.r, self.m, self.z
-        first, second = self.parts(kind, p, z, self.d)
+    def own(self, kind, p, d=None):
+        r, z = self.r, self.z
+        d = self.d if d is None else d
+        m = d - self.base
+        first, second = self.parts(kind, p, z, d)
         if kind == "A":
             n = r.D // GROUP // 2
             k = r.W // GROUP // 2
@@ -329,46 +338,73 @@
         def _():
             src, dst = zip(*self.own(kind, p))
             to = 2 - z // 3 if i == 2 else 1 + z // 3
-            self.send(src, dst, self.r.rz.at[self.index(kind, p, i)], (d, to))
+            sem = self.r.rz.at[self.index(kind, p, i)]
+            self.send(src, dst, sem, (d, to))
+            if kind == "B" and i == 3:
+                for n, wide in ((0, "X"), (1, "Y")):
+
+                    @pl.when(p % 2 == n)
+                    def _():
+                        src, dst = zip(*self.own("B", p, self.pair(wide)[0]))
+                        self.send(src, dst, sem, (d, to))
 
     def z_stage(self, t):
-        self.wait(64, self.r.rz.at[t])
-
         def forward(kind, p, i):
-            @pl.when(self.inner & (i < 3))
-            def _():
-                piece = self.parts(kind, p, self.quarter(i), self.d)
-                self.send(piece, piece, self.r.rz.at[self.index(kind, p, i + 1)], (self.d, 3 * (self.z - 1)))
+            self.wait(128 if kind in "XY" else 64, self.r.rz.at[t])
+            if kind in "AB":
+
+                @pl.when(self.inner & (i < 3))
+                def _():
+                    piece = self.parts(kind, p, self.quarter(i), self.d)
+                    self.send(piece, piece, self.r.rz.at[self.index(kind, p, i + 1)], (self.d, 3 * (self.z - 1)))
 
         self.unit(t, forward)
 
     def xy_sends(self, t):
         def go(kind, p, i):
-            z, r = self.z, self.r
-            piece = self.parts(kind, p, self.quarter(i), self.d)
-            self.send(piece, piece, r.rx.at[t], (self.dx, z))
-            self.send(piece, piece, r.ry.at[t], (self.dy, z))
-            self.send(piece, piece, r.rs.at[t], (self.ds, z))
+            z, r, q = self.z, self.r, self.quarter(i)
+            if kind in "AB":
+                carried, targets = (self.d,), ((r.rx, self.dx), (r.ry, self.dy))
+            else:
+                beside, across = self.pair(kind)
+                carried, targets = (self.d, beside), (((r.rx if kind == "X" else r.ry), across),)
+            for frm in carried:
+                piece = self.parts(kind, p, q, frm)
+                for sem, to in targets + ((r.rs, self.ds),):
+                    self.send(piece, piece, sem.at[t], (to, z))
 
         self.unit(t, go)
 
     def xy_stage(self, t):
         def go(kind, p, i):
             z, q, r = self.z, self.quarter(i), self.r
+            if kind in "XY":
+                self.wait(128, (r.rx if kind == "X" else r.ry).at[t])
+                for frm in (self.pair(kind)[1], self.dd):
+                    w = self.parts(kind, p, q, frm)
+                    self.send(w, w, r.rs.at[t], (self.ds, z))
+                return
             for sem, frm, to, half in ((r.rx, self.dx, self.dy, 0), (r.ry, self.dy, self.dx, 1)):
                 self.wait(64, sem.at[t])
                 h = self.parts(kind, p, q, frm, half)
                 self.send(h, h, r.rd.at[t], (to, z))
                 w = self.parts(kind, p, q, frm)
                 self.send(w, w, r.rs.at[t], (self.ds, z))
+                if kind == "B":
+                    n = 0 if to is self.dx else 1
+
+                    @pl.when(self.inner & (i == 2) & (p % 2 == n))
+                    def _():
+                        self.send(w, w, r.rz.at[self.index("B", p, 3)], (self.d, 3 * (z - 1)))
 
         self.unit(t, go)
 
     def d_stage(self, t):
         def go(kind, p, i):
-            self.wait(64, self.r.rd.at[t])
-            w = self.parts(kind, p, self.quarter(i), self.dd)
-            self.send(w, w, self.r.rs.at[t], (self.ds, self.z))
+            if kind in "AB":
+                self.wait(64, self.r.rd.at[t])
+                w = self.parts(kind, p, self.quarter(i), self.dd)
+                self.send(w, w, self.r.rs.at[t], (self.ds, self.z))
 
         self.unit(t, go)
 
@@ -377,7 +413,7 @@
 
     def finish_sends(self):
         kinds = 6
-        always = 7 * self.n + 2 * kinds
+        always = 7 * self.n - 4 + 2 * kinds + 4
 
         @pl.loop(0, jnp.where(self.inner, always + 2 * kinds, always))
         def _(i):
@@ -463,7 +499,9 @@
     r.before, r.gh = r.st.at[:, pl.ds(0, STEP)], r.st.at[:, pl.ds(STEP, STEP)]
     r.hidden, r.gb = r.ds.at[:, pl.ds(0, STEP)], r.ds.at[:, pl.ds(STEP, STEP)]
     r.ga = r.branch
-    r.out, r.gin = r.second, r.first
+    r.outq, r.gin = r.dzq, r.first
+    for k, name in enumerate(("aqd", "aou", "a1d", "a2u")):
+        setattr(r, name, r.dense.at[:, pl.ds(k * r.D, r.D)])
     r.length = r.len[z]
     r.my_ids = [r.ids[z, p] for p in range(4)]
     c.greet()
@@ -557,7 +595,7 @@
                 ).start()
 
     N = c.n
-    LZ, LX, LD = 2, 1, 1
+    LZ, LX, LD = 1, 1, 1
     lag = LZ + LX + LD
     c.inner_sends("A", 0)
     c.inner_sends("A", 1)
@@ -573,7 +611,7 @@
         pl.when((t >= LZ + LX) & (t < LZ + LX + N))(lambda: c.d_stage(t - LZ - LX))
         pl.when(t >= lag)(lambda: c.s_stage(t - lag))
         pl.when(t + 1 < N)(lambda: c.z_stage(t + 1))
-        pl.when(t < 4)(lambda: c.inner_sends("B", t))
+        pl.when((t >= 1) & (t < 5))(lambda: c.inner_sends("B", t - 1))
 
         @pl.when((t == 0) | (t == 2))
         def _():
@@ -581,9 +619,9 @@
                 pl.when(t == 0)(lambda: c.outer_sends("A", p, 2))
                 pl.when(t == 2)(lambda: c.outer_sends("A", p, 3))
 
-        pl.when((t >= 2) & (t < 6))(lambda: c.outer_sends("B", t - 2, 2))
-        pl.when((t >= 6) & (t < 10))(lambda: c.outer_sends("B", t - 6, 3))
-        pl.when((t >= 3) & (t < 3 + 2 * CUTS) & (t % 2 == 1))(lambda: send_cot((t - 3) // 2))
+        pl.when((t >= 4) & (t < 8))(lambda: c.outer_sends("B", t - 4, 2))
+        pl.when((t >= 9) & (t < 13))(lambda: c.outer_sends("B", t - 9, 3))
+        pl.when((t >= 2) & (t < 2 + 2 * CUTS) & (t % 2 == 0))(lambda: send_cot((t - 2) // 2))
         pl.when(t == 0)(pick_first)
         pl.when(t == 1)(pick_attn)
         pl.when(t == 2)(lambda: wait_all(l_q))
@@ -592,21 +630,18 @@
         pl.when(t == 9)(send_f1)
         pl.when(t == 11)(send_f2)
         pl.when(t == 1 + lag)(have_attn)
-        pl.when((t == 2) | (t == 1 + lag) | (t == 3 + lag) | (t == 5 + lag))(lambda: attn_fwd(r, c.quarter((t - 2) // 2)))
+        pl.when((t == 2) | (t == 1 + lag) | (t == 3 + lag) | (t == 5 + lag))(lambda: attn_fwd(r, c.quarter((t - 1) // 2)))
 
         @pl.when(t == 5 + lag)
         def _():
             after_attn(r)
             wait_all(l_f)
 
-        pl.when(t == 13)(have_cot)
-        pl.when(t == 15)(have_ffn)
-        pl.when((t >= 13) & (t != 20))(lambda: ffn(jnp.minimum(t - 13, 7)))
+        pl.when(t == 12)(have_cot)
+        pl.when(t == 14)(have_ffn)
+        pl.when((t >= 12) & (t != 19))(lambda: ffn(jnp.minimum(t - 12, 7)))
 
     mine = block_of(z, W)
-
-    def cut(ref):
-        return lambda j: ref.at[:, block_of(j, W)]
 
     def group(lo, own_end, hi, s, fs, fr, out=None):
         cols, own, reps, zc = pl.ds(lo, hi - lo), pl.ds(lo, own_end - lo), pl.ds(own_end, hi - own_end), pl.ds(fr, hi - own_end)
@@ -684,11 +719,17 @@
                     src_ref=src, dst_ref=dst, send_sem=r.misc.at[36], recv_sem=r.misc.at[37], device_id=(d, q), device_id_type=MESH
                 ).start()
 
+    def send_out(k):
+        rows = pl.ds(k * (S // 2), S // 2)
+        c.to_planes(lambda j: r.outq.at[j, rows, :], r.outr.at[z, rows, :], r.misc.at[4], r.misc.at[5])
+        fetch(lambda: (r.outq.at[z, rows, :], r.outr.at[z, rows, :]))
+
+    r.lift_fc2[...] = r.lift_fc2_acc[...].astype(BF)
+    after_ffn_out(r)
+    send_out(0)
     after_ffn_back(r)
     m_send([(r.g_f1d, W, m0), (r.g_f2u, W, m0 + W), (r.g_ou, W, m0 + 2 * W)])
-    after_ffn_out(r)
-    c.to_planes(cut(r.out), r.outr.at[z], r.misc.at[4], r.misc.at[5])
-    fetch(lambda: (r.out.at[:, mine], r.outr.at[z]))
+    send_out(1)
     for ref, base in ((r.g_f1, 0), (r.g_f2, FQ)):
         r.sp[z, :, base : base + FQ] = ref[:, block_of(z, FQ)]
     back_attended(r)
@@ -816,8 +857,7 @@
         heads = W // HD
         vm = dict(
             wq=((4, D, 3 * W), BF), wo=((4, W, D), BF), w1=((4, D, FQ), BF), w2=((4, FQ, D), BF),
-            aqd=((T, D), BF), aqu=((A, 3, R, W), BF), aod=((T, W), BF), a1u=((T, FQ), BF), a2d=((T, FQ), BF),
-            aou=((T, D), BF), a1d=((T, D), BF), a2u=((T, D), BF),
+            aqu=((A, 3, R, W), BF), aod=((T, W), BF), a1u=((T, FQ), BF), a2d=((T, FQ), BF),
             out_qu=((n, R, 3 * W), BF), out_od=((n, R, W), BF), out_f1=((n, R, FQ), BF), out_f2=((n, R, FQ), BF),
             sel_qu=((R, 12 * W), BF), sel_od=((R, 4 * W), BF), sel_f1=((R, 4 * FQ), BF), sel_f2=((R, 4 * FQ), BF),
             dn_qkv=((R, D), BF), up_out=((R, D), BF), dn_fc1=((R, D), BF), up_fc2=((R, D), BF),

time: 153 us -> 149 us (0.974)
  Pallas kernels: 152 us -> 148 us
    pallas_call x1, Pallas kernels: 148 us -> 144 us  [shards(): pl.pallas_call(lambda *refs: kernel(names, sizes, *refs), out_shape=tuple...]
where the time goes in v3:
time: 149 us
  Pallas kernels  148 us (99%)
    pallas_call x1, Pallas kernels, shards(): pl.pallas_call(lambda *refs: kernel(names, sizes, *refs), out_shape=tuple...  144 us
    pallas_call x1, Pallas kernels, shards(): pl.pallas_call(lambda *refs: spread(names, *refs), out_shape=tuple((jax.S...  3.95 us

profile of v3, /device:TPU:0, one launch (start us, length us, event | category | flops | bytes accessed | tf_op | source)
XLA Modules:
  0.0 149.1 jit_solution(16111238893504682774)
XLA Ops:
  0.6 144.3 %shard_map.231 = (bf16[4,320,256]{2,1,0:T(8,128)(2,1)}, bf16[4,320,256]{2,1,0:T(8,128)(2,1)}, bf16[8,16,3072]{2,1,0:T(8,128)(2,1)}, bf16[8,4,16,768]{3,2,1,0:T(8,128)(2,1)}, bf16[8,16,1024]{2,1,0:T(8,128)(2,1)}) custom-call(s32[4]{0:T(128)} %refs_0_.1, s32[4,4]{1,0:T(4,128)} %refs_1_.1, bf16[4,320,1024]{2,1,0:T(8,128)(2,1)} %refs_2_.1, ...), custom_call_target="tpu_custom_call" | custom-call | tf_op jit(solution)/shard_map/pallas_call | solution.py:880
  145.0 4.0 %shard_map.232 = (f32[4,320,256]{2,1,0:T(8,128)}, f32[4,320,256]{2,1,0:T(8,128)}, f32[8,16,1024]{2,1,0:T(8,128)}, f32[8,3,16,256]{3,2,1,0:T(8,128)}, f32[8,16,25...) custom-call(bf16[4,320,256]{2,1,0:T(8,128)(2,1)} %get-tuple-element., ...), custom_call_target="tpu_custom_call" | custom-call | tf_op jit(solution)/shard_map/pallas_call | solution.py:899

commit v4 on v3

--- a/solution.py
+++ b/solution.py
@@ -613,15 +613,15 @@
         pl.when(t + 1 < N)(lambda: c.z_stage(t + 1))
         pl.when((t >= 1) & (t < 5))(lambda: c.inner_sends("B", t - 1))
 
-        @pl.when((t == 0) | (t == 2))
+        @pl.when((t == 0) | (t == 3))
         def _():
             for p in range(2):
                 pl.when(t == 0)(lambda: c.outer_sends("A", p, 2))
-                pl.when(t == 2)(lambda: c.outer_sends("A", p, 3))
-
-        pl.when((t >= 4) & (t < 8))(lambda: c.outer_sends("B", t - 4, 2))
-        pl.when((t >= 9) & (t < 13))(lambda: c.outer_sends("B", t - 9, 3))
-        pl.when((t >= 2) & (t < 2 + 2 * CUTS) & (t % 2 == 0))(lambda: send_cot((t - 2) // 2))
+                pl.when(t == 3)(lambda: c.outer_sends("A", p, 3))
+
+        pl.when((t >= 5) & (t < 9))(lambda: c.outer_sends("B", t - 5, 2))
+        pl.when((t >= 10) & (t < 14))(lambda: c.outer_sends("B", t - 10, 3))
+        pl.when((t >= 1) & (t < 11) & ((t - 1) % 2 == 0))(lambda: send_cot((t - 1) // 2))
         pl.when(t == 0)(pick_first)
         pl.when(t == 1)(pick_attn)
         pl.when(t == 2)(lambda: wait_all(l_q))
@@ -754,10 +754,10 @@
         c.to_planes(lambda j: r.gin.at[rows, block_of(j, W)], r.ginr.at[z, rows, :], r.misc.at[6], r.misc.at[7])
         fetch(lambda: (r.gin.at[rows, mine], r.ginr.at[z, rows, :]))
 
+    finish_rows(r, 0)
+    send_gin(0)
     p_expand()
     l_expand()
-    finish_rows(r, 0)
-    send_gin(0)
     finish_rows(r, 1)
     send_gin(1)
     e_relay()
@@ -793,32 +793,43 @@
         stores.append(pltpu.make_async_copy(getattr(r, "v_" + key), getattr(r, "o_" + key), r.sem_out.at[len(stores)]))
         stores[-1].start()
 
-    def widen(ref, value):
-        ref[...] = value.astype(F32)
+    def widen(ref, src):
+        @pl.loop(0, ref.shape[0])
+        def _(i):
+            ref[i] = src(i).astype(F32)
 
     loads[0].wait()
-    widen(r.v_out, r.b_out[...])
+    widen(r.v_out, lambda i: r.b_out[i])
     store("out")
     loads[1].wait()
-    widen(r.v_gin, r.b_gin[...])
+    widen(r.v_gin, lambda i: r.b_gin[i])
     store("gin")
     loads[2].wait()
-    widen(r.v_f1u, r.b_s[:, :, :FQ])
+    widen(r.v_f1u, lambda i: r.b_s[i, :, :FQ])
     store("f1u")
-    widen(r.v_f2d, r.b_s[:, :, FQ : 2 * FQ])
+    widen(r.v_f2d, lambda i: r.b_s[i, :, FQ : 2 * FQ])
     store("f2d")
-    for i in range(3):
-        r.v_qu[:, i] = r.b_s[:, :, 2 * FQ + i * W : 2 * FQ + (i + 1) * W].astype(F32)
+
+    @pl.loop(0, r.v_qu.shape[0])
+    def _(i):
+        for k in range(3):
+            r.v_qu[i, k] = r.b_s[i, :, 2 * FQ + k * W : 2 * FQ + (k + 1) * W].astype(F32)
+
     store("qu")
-    widen(r.v_od, r.b_s[:, :, 2 * FQ + 3 * W :])
+    widen(r.v_od, lambda i: r.b_s[i, :, 2 * FQ + 3 * W :])
     store("od")
     loads[3].wait()
     for k, key in enumerate(("f1d", "f2u", "ou")):
-        for j in range(4):
-            getattr(r, "v_" + key)[:, :, W * j : W * (j + 1)] = r.b_r[:, j, :, W * k : W * (k + 1)].astype(F32)
+        ref = getattr(r, "v_" + key)
+
+        @pl.loop(0, ref.shape[0])
+        def _(i):
+            for j in range(4):
+                ref[i, :, W * j : W * (j + 1)] = r.b_r[i, j, :, W * k : W * (k + 1)].astype(F32)
+
         store(key)
     loads[4].wait()
-    widen(r.v_qd, r.b_p[...])
+    widen(r.v_qd, lambda i: r.b_p[i])
     store("qd")
     for cp in stores:
         cp.wait()

time: 149 us -> 146 us (0.980)
  Pallas kernels: 148 us -> 145 us
    pallas_call x1, Pallas kernels: 144 us -> 141 us  [shards(): pl.pallas_call(lambda *refs: kernel(names, sizes, *refs), out_shape=tuple...]
where the time goes in v4:
time: 146 us
  Pallas kernels  145 us (99%)
    pallas_call x1, Pallas kernels, shards(): pl.pallas_call(lambda *refs: kernel(names, sizes, *refs), out_shape=tuple...  141 us
    pallas_call x1, Pallas kernels, shards(): pl.pallas_call(lambda *refs: spread(names, *refs), out_shape=tuple((jax.S...  3.96 us

profile of v4, /device:TPU:0, one launch (start us, length us, event | category | flops | bytes accessed | tf_op | source)
XLA Modules:
  0.0 146.3 jit_solution(15416287523675578749)
XLA Ops:
  0.6 141.5 %shard_map.231 = (bf16[4,320,256]{2,1,0:T(8,128)(2,1)}, bf16[4,320,256]{2,1,0:T(8,128)(2,1)}, bf16[8,16,3072]{2,1,0:T(8,128)(2,1)}, bf16[8,4,16,768]{3,2,1,0:T(8,128)(2,1)}, bf16[8,16,1024]{2,1,0:T(8,128)(2,1)}) custom-call(s32[4]{0:T(128)} %refs_0_.1, s32[4,4]{1,0:T(4,128)} %refs_1_.1, bf16[4,320,1024]{2,1,0:T(8,128)(2,1)} %refs_2_.1, ...), custom_call_target="tpu_custom_call" | custom-call | tf_op jit(solution)/shard_map/pallas_call | solution.py:891
  142.1 4.0 %shard_map.232 = (f32[4,320,256]{2,1,0:T(8,128)}, f32[4,320,256]{2,1,0:T(8,128)}, f32[8,16,1024]{2,1,0:T(8,128)}, f32[8,3,16,256]{3,2,1,0:T(8,128)}, f32[8,16,25...) custom-call(bf16[4,320,256]{2,1,0:T(8,128)(2,1)} %get-tuple-element., ...), custom_call_target="tpu_custom_call" | custom-call | tf_op jit(solution)/shard_map/pallas_call | solution.py:910

commit v5 on v4

--- a/solution.py
+++ b/solution.py
@@ -255,10 +255,10 @@
 
     def unit(self, t, f):
         pl.when(t < self.n_a)(lambda: f("A", t % 2, t // 2 + 1))
-        pl.when((t >= self.n_a) & (t < self.n - 4))(lambda: f("B", (t - self.n_a) % 4, (t - self.n_a) // 4 + 1))
-        last = t - (self.n - 4)
-        pl.when((last >= 0) & (last % 2 == 0))(lambda: f("X", last, 3))
-        pl.when((last >= 0) & (last % 2 == 1))(lambda: f("Y", last, 3))
+        pl.when((t >= self.n_a) & (t < self.n - 2))(lambda: f("B", (t - self.n_a) % 4, (t - self.n_a) // 4 + 1))
+        last = t - (self.n - 2)
+        pl.when((last >= 0) & (last % 2 == 0))(lambda: f("X", last + 2, 3))
+        pl.when((last >= 0) & (last % 2 == 1))(lambda: f("Y", last + 2, 3))
 
     def pair(self, kind):
         return (self.dy, self.dx) if kind == "X" else (self.dx, self.dy)
@@ -343,7 +343,7 @@
             if kind == "B" and i == 3:
                 for n, wide in ((0, "X"), (1, "Y")):
 
-                    @pl.when(p % 2 == n)
+                    @pl.when(p == n + 2)
                     def _():
                         src, dst = zip(*self.own("B", p, self.pair(wide)[0]))
                         self.send(src, dst, sem, (d, to))
@@ -393,7 +393,7 @@
                 if kind == "B":
                     n = 0 if to is self.dx else 1
 
-                    @pl.when(self.inner & (i == 2) & (p % 2 == n))
+                    @pl.when(self.inner & (i == 2) & (p == n + 2))
                     def _():
                         self.send(w, w, r.rz.at[self.index("B", p, 3)], (self.d, 3 * (z - 1)))
 
@@ -413,7 +413,7 @@
 
     def finish_sends(self):
         kinds = 6
-        always = 7 * self.n - 4 + 2 * kinds + 4
+        always = 7 * self.n - 2 + 2 * kinds + 2
 
         @pl.loop(0, jnp.where(self.inner, always + 2 * kinds, always))
         def _(i):
@@ -784,9 +784,11 @@
     W = r.b_out.shape[2]
     FQ = r.v_f1u.shape[2]
     loads = []
-    for k, (src, dst) in enumerate(((r.outr, r.b_out), (r.ginr, r.b_gin), (r.fin_s, r.b_s), (r.fin_r, r.b_r), (r.fin_p, r.b_p))):
+    pieces = [(ref.at[i], buf.at[i]) for ref, buf in ((r.outr, r.b_out), (r.ginr, r.b_gin)) for i in range(r.b_out.shape[0])]
+    for k, (src, dst) in enumerate(pieces + [(r.fin_s, r.b_s), (r.fin_r, r.b_r), (r.fin_p, r.b_p)]):
         loads.append(pltpu.make_async_copy(src, dst, r.sem_in.at[k]))
         loads[-1].start()
+    images = r.b_out.shape[0]
     stores = []
 
     def store(key):
@@ -798,12 +800,14 @@
         def _(i):
             ref[i] = src(i).astype(F32)
 
-    loads[0].wait()
-    widen(r.v_out, lambda i: r.b_out[i])
-    store("out")
-    loads[1].wait()
-    widen(r.v_gin, lambda i: r.b_gin[i])
-    store("gin")
+    for j, key in enumerate(("out", "gin")):
+        for i in range(images):
+            loads[j * images + i].wait()
+            wide = getattr(r, "v_" + key)
+            wide[i] = getattr(r, "b_" + key)[i].astype(F32)
+            stores.append(pltpu.make_async_copy(wide.at[i], getattr(r, "o_" + key).at[i], r.sem_out.at[len(stores)]))
+            stores[-1].start()
+    loads = loads[2 * images - 2 :]
     loads[2].wait()
     widen(r.v_f1u, lambda i: r.b_s[i, :, :FQ])
     store("f1u")
@@ -914,7 +918,7 @@
             out_specs=tuple([anywhere] * len(wide)),
             scratch_shapes=[pltpu.VMEM(v.shape, v.dtype) for v in held.values()]
             + [pltpu.VMEM(v, F32) for v in wide.values()]
-            + [pltpu.SemaphoreType.DMA((5,)), pltpu.SemaphoreType.DMA((len(wide),))],
+            + [pltpu.SemaphoreType.DMA((2 * n + 3,)), pltpu.SemaphoreType.DMA((2 * n + 8,))],
             compiler_params=pltpu.CompilerParams(vmem_limit_bytes=60 * 2**20),
         )(outr, ginr, fin_s, fin_r, fin_p)
         back = lambda a: jnp.transpose(a, (0, 2, 1))

time: 146 us -> 146 us (level)
  no operation moved by 1% of the time
where the time goes in v5:
time: 146 us
  Pallas kernels  145 us (99%)
    pallas_call x1, Pallas kernels, shards(): pl.pallas_call(lambda *refs: kernel(names, sizes, *refs), out_shape=tuple...  142 us
    pallas_call x1, Pallas kernels, shards(): pl.pallas_call(lambda *refs: spread(names, *refs), out_shape=tuple((jax.S...  3.82 us

profile of v5, /device:TPU:0, one launch (start us, length us, event | category | flops | bytes accessed | tf_op | source)
XLA Modules:
  0.0 146.2 jit_solution(934766120432788259)
XLA Ops:
  0.6 141.6 %shard_map.231 = (bf16[4,320,256]{2,1,0:T(8,128)(2,1)}, bf16[4,320,256]{2,1,0:T(8,128)(2,1)}, bf16[8,16,3072]{2,1,0:T(8,128)(2,1)}, bf16[8,4,16,768]{3,2,1,0:T(8,128)(2,1)}, bf16[8,16,1024]{2,1,0:T(8,128)(2,1)}) custom-call(s32[4]{0:T(128)} %refs_0_.1, s32[4,4]{1,0:T(4,128)} %refs_1_.1, bf16[4,320,1024]{2,1,0:T(8,128)(2,1)} %refs_2_.1, ...), custom_call_target="tpu_custom_call" | custom-call | tf_op jit(solution)/shard_map/pallas_call | solution.py:895
  142.2 3.8 %shard_map.232 = (f32[4,320,256]{2,1,0:T(8,128)}, f32[4,320,256]{2,1,0:T(8,128)}, f32[8,16,1024]{2,1,0:T(8,128)}, f32[8,3,16,256]{3,2,1,0:T(8,128)}, f32[8,16,25...) custom-call(bf16[4,320,256]{2,1,0:T(8,128)(2,1)} %get-tuple-element., ...), custom_call_target="tpu_custom_call" | custom-call | tf_op jit(solution)/shard_map/pallas_call | solution.py:914

commit v6 on v5

--- a/solution.py
+++ b/solution.py
@@ -190,9 +190,11 @@
 def back_attended(r):
     W = r.W
     r.ga[...] = dot(r.g_out[...], r.sel_od[...])
-    for q in range(4):
-        c = slice(q * W, (q + 1) * W)
-        r.ga[:, c] += dot_nt(r.gbr[...], r.wo[q])
+
+    @pl.loop(0, 4)
+    def _(q):
+        r.ga[:, block_of(q, W)] += dot_nt(r.gbr[...], r.wo[q])
+
     r.g_od[...] = dot_tn(r.g_out[...], r.att[...]).astype(BF)
 
 
@@ -227,8 +229,10 @@
 def back_first(r):
     W = r.W
     r.mixed[...] = dot(r.g_qkv[...], r.dn_qkv[...])
-    for q in range(4):
-        r.mixed[...] += dot_nt(r.gp[:, 3 * W * q : 3 * W * (q + 1)], r.wq[q])
+
+    @pl.loop(0, 4)
+    def _(q):
+        r.mixed[...] += dot_nt(r.gp[:, block_of(q, 3 * W)], r.wq[q])
 
 
 def finish_rows(r, k):

time: 146 us -> 147 us (level)
  no operation moved by 1% of the time
where the time goes in v6:
time: 147 us
  Pallas kernels  146 us (99%)
    pallas_call x1, Pallas kernels, shards(): pl.pallas_call(lambda *refs: kernel(names, sizes, *refs), out_shape=tuple...  142 us
    pallas_call x1, Pallas kernels, shards(): pl.pallas_call(lambda *refs: spread(names, *refs), out_shape=tuple((jax.S...  3.82 us

profile of v6, /device:TPU:0, one launch (start us, length us, event | category | flops | bytes accessed | tf_op | source)
XLA Modules:
  0.0 146.6 jit_solution(8290220233962405953)
XLA Ops:
  0.6 142.1 %shard_map.231 = (bf16[4,320,256]{2,1,0:T(8,128)(2,1)}, bf16[4,320,256]{2,1,0:T(8,128)(2,1)}, bf16[8,16,3072]{2,1,0:T(8,128)(2,1)}, bf16[8,4,16,768]{3,2,1,0:T(8,128)(2,1)}, bf16[8,16,1024]{2,1,0:T(8,128)(2,1)}) custom-call(s32[4]{0:T(128)} %refs_0_.1, s32[4,4]{1,0:T(4,128)} %refs_1_.1, bf16[4,320,1024]{2,1,0:T(8,128)(2,1)} %refs_2_.1, ...), custom_call_target="tpu_custom_call" | custom-call | tf_op jit(solution)/shard_map/pallas_call | solution.py:899
  142.8 3.8 %shard_map.232 = (f32[4,320,256]{2,1,0:T(8,128)}, f32[4,320,256]{2,1,0:T(8,128)}, f32[8,16,1024]{2,1,0:T(8,128)}, f32[8,3,16,256]{3,2,1,0:T(8,128)}, f32[8,16,25...) custom-call(bf16[4,320,256]{2,1,0:T(8,128)(2,1)} %get-tuple-element., ...), custom_call_target="tpu_custom_call" | custom-call | tf_op jit(solution)/shard_map/pallas_call | solution.py:918
